TPU v7x, 128 devices: a whole 4x4x4 slice. The times are simulated.
128 devices in a mesh: tm: 8 (over x, z_hi), space: 16 (over y, z_lo, core).
Axes of the slice: x: 4, y: 4, z: 4 (z_hi: 2, z_lo: 2; z = z_hi * 2 + z_lo), core: 2. Of those that a mesh axis runs over, the one named last changes fastest.
Arguments:
- initial: float32 [4, 64, 16, 128], P(None, None, 'space'), may hold values from -6 to 6
- neighbours: int32 [6, 16, 128], P(None, 'space'), may hold values from 0 to 127, as said below
- step_counts: int32 [8], P('tm'), may hold values from 1 to 3
Outputs:
- node_states: float32 [8, 3, 4, 64, 16, 128], P('tm', None, None, None, 'space')
Inputs may be any that keep to these rules, and one draw needn't show every extreme that they name: neighbours[f, i, e] is the element that shares face f (order -x, +x, -y, +y, -z, +z) with element e of layer i: an index in layer i-1 (f = 0) or i+1 (f = 1), periodic over 16 layers, or in layer i (f = 2..5). The elements of each layer form a periodic 8 x 16 grid, numbered in an order of that layer's own; the relation is symmetric and all elements keep the same orientation.
All inputs are finite; a program needn't handle non-finite values.
Results may differ from a plain program's by a relative error of at most 0.00014.
Values sent between devices are 32-bit elements; how exact they have to be, the bound alone decides.
No kernel may reach another device: no remote copies, remote signals or barrier semaphores. Data moves between devices by JAX's collectives and lax.ppermute only.
A program may use at most 64 MiB of HBM per device.

v0:
```python
import jax
import jax.numpy as jnp
import numpy as np
from jax import lax
from jax.sharding import PartitionSpec as P

ORDER = 4
NODES = 64
ITERS = 2


LIFT_FACTOR = 6.0
BASE_STEP = 0.015


def from_behind(block, axis, distance):
    devices = range(lax.axis_size(axis))
    route = [((i - distance) % len(devices), i) for i in devices]
    return lax.ppermute(block, axis, route)


def from_behind_2(value, axis, steps):
    count = lax.axis_size(axis)
    initial, last = (max(0, -steps), min(count, count - steps))
    return lax.ppermute(value, axis, [(source, source + steps) for source in range(initial, last)])


def derivative_table():
    points = np.array([-1.0, -1.0 / np.sqrt(5.0), 1.0 / np.sqrt(5.0), 1.0])
    node_count = points.shape[0]
    weights = np.zeros(node_count)
    for row_index in range(node_count):
        product = 1.0
        for col_index in range(node_count):
            if col_index != row_index:
                product = product * (points[row_index] - points[col_index])
        weights[row_index] = 1.0 / product
    table = np.zeros((node_count, node_count))
    for row_index in range(node_count):
        for col_index in range(node_count):
            if col_index != row_index:
                table[row_index, col_index] = (
                    weights[col_index]
                    / weights[row_index]
                    / (points[row_index] - points[col_index])
                )
        table[row_index, row_index] = -np.sum(table[row_index])
    return table


def build_tables():
    small = derivative_table()
    identity = np.eye(ORDER)
    deriv_x = np.kron(np.kron(small, identity), identity)
    deriv_y = np.kron(np.kron(identity, small), identity)
    deriv_z = np.kron(np.kron(identity, identity), small)
    first_idx = np.arange(ORDER)[:, None]
    second_idx = np.arange(ORDER)[None, :]
    last = ORDER - 1
    inside_lists = [
        (4 * first_idx + second_idx).reshape(-1),
        (16 * last + 4 * first_idx + second_idx).reshape(-1),
        (16 * first_idx + second_idx).reshape(-1),
        (16 * first_idx + 4 * last + second_idx).reshape(-1),
        (16 * first_idx + 4 * second_idx).reshape(-1),
        (16 * first_idx + 4 * second_idx + last).reshape(-1),
    ]
    outside_lists = [None, None, inside_lists[3], inside_lists[2], inside_lists[5], inside_lists[4]]
    quarter = ORDER * ORDER
    lifting = np.zeros((ORDER**3, 6 * quarter))
    for face in range(6):
        for row in range(quarter):
            lifting[inside_lists[face][row], face * quarter + row] = 1.0
    return (deriv_x, deriv_y, deriv_z, inside_lists, outside_lists, lifting)


def node_product(matrix, value):
    return jnp.einsum("mn,kne->kme", matrix, value, precision=lax.Precision.HIGHEST)


def apply_operator(field, low_outside, high_outside, flat_index, tables):
    deriv_x, deriv_y, deriv_z, inside_lists, outside_lists, lifting = tables
    quarter = ORDER * ORDER
    pressure = field[:, 0]
    rate_p = -(
        node_product(deriv_x, field[:, 1])
        + node_product(deriv_y, field[:, 2])
        + node_product(deriv_z, field[:, 3])
    )
    rate_u = [
        -node_product(deriv_x, pressure),
        -node_product(deriv_y, pressure),
        -node_product(deriv_z, pressure),
    ]
    p_terms = []
    u_terms = []
    for face in range(6):
        sign = -1.0 if face % 2 == 0 else 1.0
        direction = face // 2 + 1
        inside = jnp.take(field, inside_lists[face], axis=2)
        if face == 0:
            source = low_outside
        elif face == 1:
            source = high_outside
        else:
            source = jnp.take(field, outside_lists[face], axis=2)
        outside = jnp.take(source, flat_index[face], axis=3)
        jump_p = inside[:, 0] - outside[:, 0]
        jump_u = sign * (inside[:, direction] - outside[:, direction])
        p_terms.append(0.5 * LIFT_FACTOR * (jump_u - jump_p))
        u_terms.append(sign * 0.5 * LIFT_FACTOR * (jump_p - jump_u))
    rate_p = rate_p + node_product(lifting, jnp.concatenate(p_terms, axis=1))
    rates = [rate_p]
    for direction in range(3):
        part_lift = lifting[:, 2 * direction * quarter : (2 * direction + 2) * quarter]
        both = jnp.concatenate([u_terms[2 * direction], u_terms[2 * direction + 1]], axis=1)
        rates.append(rate_u[direction] + node_product(part_lift, both))
    return jnp.stack(rates, axis=1)


def images(field, flat_index, tables, layers, cells):
    quarter = NODES // ORDER
    upper_face = field[:, :, NODES - quarter :]
    lower_face = field[:, :, :quarter]
    arrived_low = from_behind(upper_face[:, :, :, (layers - 1) * cells :], "space", 1)
    arrived_high = from_behind(lower_face[:, :, :, :cells], "space", -1)
    low_outside = jnp.concatenate(
        [arrived_low, upper_face[:, :, :, : (layers - 1) * cells]], axis=3
    )
    high_outside = jnp.concatenate([lower_face[:, :, :, cells:], arrived_high], axis=3)
    return apply_operator(field, low_outside, high_outside, flat_index, tables)


def shards(initial, neighbours, step_counts):
    raw = build_tables()
    tables = (
        jnp.asarray(raw[0], jnp.float32),
        jnp.asarray(raw[1], jnp.float32),
        jnp.asarray(raw[2], jnp.float32),
        raw[3],
        raw[4],
        jnp.asarray(raw[5], jnp.float32),
    )
    fields, nodes, layers, cells = initial.shape
    offsets = (jnp.arange(layers, dtype=jnp.int32) * cells)[None, :, None]
    flat_index = (neighbours + offsets).reshape(6, layers * cells)
    step = step_counts.astype(jnp.float32)[0] * BASE_STEP
    first_slice = lax.axis_index("tm") == 0
    anchor = initial.reshape(1, fields, nodes, layers * cells)
    states = jnp.broadcast_to(anchor, (3, fields, nodes, layers * cells))

    def apply_all(value):
        return images(value, flat_index, tables, layers, cells)

    for iteration in range(ITERS):
        old = apply_all(states)
        start = states[0:1]
        first = start + step * (
            5.0 / 24.0 * old[0:1] + 1.0 / 3.0 * old[1:2] - 1.0 / 24.0 * old[2:3]
        )
        image_first = apply_all(first)
        second = (
            first
            + step * (image_first - old[1:2])
            + step * (-1.0 / 24.0 * old[0:1] + 1.0 / 3.0 * old[1:2] + 5.0 / 24.0 * old[2:3])
        )
        image_second = apply_all(second)
        correction = step * (
            2.0 / 3.0 * image_first - 1.0 / 3.0 * old[0:1] - 1.0 / 3.0 * image_second
        )
        carried = step * (0.5 * image_second - 0.5 * old[0:1]) + correction

        def section(turn, carry):
            previous_end, begin_old = carry
            arrived = from_behind_2(previous_end, "tm", 1)
            begin = jnp.where(first_slice, anchor, arrived)
            begin_image = apply_all(begin)
            middle = begin + step * begin_image + carried
            middle_image = apply_all(middle)
            finish = begin + 0.5 * step * (begin_image + middle_image) + correction
            return (finish, begin)

        new_end, new_start = lax.fori_loop(0, lax.axis_size("tm"), section, (second, start))
        middle_state = first + 0.5 * (new_start - start + (new_end - second))
        states = jnp.concatenate([new_start, middle_state, new_end], axis=0)
    return states.reshape(1, 3, fields, nodes, layers, cells)


def solution(mesh):
    placed = (P(None, None, "space", None), P(None, "space", None), P("tm"))
    return jax.shard_map(
        shards,
        mesh=mesh,
        in_specs=placed,
        out_specs=P("tm", None, None, None, "space", None),
        check_vma=False,
    )
```

profile of v0, /device:TPU:6, one launch (start us, length us, event | category | flops | bytes accessed | tf_op | source)
XLA Modules:
  0.0 789.0 jit_solution(11732943745584859513)
XLA Ops:
  42.3 4.1 collective-permute-start.13
  79.0 318.3 %while.30 = (s32[]{:T(128)}, f32[1,4,64,128]{3,2,1,0:T(8,128)S(1)}, f32[1,4,64,128]{3,2,1,0:T(8,128)}, pred[]{:T(512)}, f32[1,4,64,128]{3,2,1,0:T(8,128)S(1)}, /...) while((s32[]{:T(128)}, f32[1,4,64,128]{3,2,1,0:T(8,128)S(1)}, ...), condition=%wide.region_1.6_spmd.clone.clone, body=%wide.region_0.5_spmd.sunk.clone.clone.sunk | while | flops 114377408 | bytes 11963442 | solution.py:183
  79.2 5.5 collective-permute-start
  116.8 4.6 collective-permute-start
  121.6 4.5 collective-permute-done
  144.9 3.9 collective-permute-start.3
  160.7 5.4 collective-permute-done
  184.9 3.9 collective-permute-start.3
  199.8 6.3 collective-permute-done
  225.0 3.9 collective-permute-start.3
  239.0 7.2 collective-permute-done
  279.1 7.2 collective-permute-done
  305.2 3.9 collective-permute-start.3
  319.2 7.2 collective-permute-done
  359.3 7.2 collective-permute-done
  385.3 3.9 collective-permute-start.3
  406.8 4.2 collective-permute-start.17
  468.3 318.3 %while.31 = (s32[]{:T(128)}, f32[1,4,64,128]{3,2,1,0:T(8,128)S(1)}, f32[1,4,64,128]{3,2,1,0:T(8,128)}, pred[]{:T(512)}, f32[1,4,64,128]{3,2,1,0:T(8,128)S(1)}, /...) while((s32[]{:T(128)}, f32[1,4,64,128]{3,2,1,0:T(8,128)S(1)}, ...), condition=%wide.region_3.8_spmd.clone.clone, body=%wide.region_2.0_spmd.sunk.clone.clone.sunk | while | flops 114377408 | bytes 11963442 | solution.py:183
  470.4 7.2 collective-permute-done.5
  508.1 7.2 collective-permute-done.5
  534.1 3.9 collective-permute-start.8
  548.4 6.9 collective-permute-done.5
  574.2 3.9 collective-permute-start.8
  588.2 7.2 collective-permute-done.5
  614.3 3.9 collective-permute-start.8
  628.3 7.2 collective-permute-done.5
  654.3 3.9 collective-permute-start.8
  668.4 7.2 collective-permute-done.5
  694.4 3.9 collective-permute-start.8
  708.5 7.2 collective-permute-done.5
  734.5 3.9 collective-permute-start.8
  748.6 7.2 collective-permute-done.5
  (2915 shorter events, 610.3 us)
Async XLA Ops:
  1.4 29.7 %collective-permute-start.11 = (f32[3,4,16,128]{3,2,1,0:T(8,128)}, f32[3,4,16,128]{3,2,1,0:T(8,128)}, u32[]{:S(2)}, u32[]{:S(2)}) collective-permute-start(f32[3,4,16,128]{3,2,1,0:T(8,128)} %broadcast_in_dim.72), channel_id=1, source_target_pairs={{1,0},{2,1},{3,2},{4,3},{5,4},{6,5},{7,6},{8,7},{9,8},{10,9},{11,1... | collective-permute-start | bytes 294920 | tf_op jit(solution)/shard_map/ppermute | solution.py:19
  5.9 22.5 %collective-permute-start.10 = (f32[3,4,16,128]{3,2,1,0:T(8,128)}, f32[3,4,16,128]{3,2,1,0:T(8,128)}, u32[]{:S(2)}, u32[]{:S(2)}) collective-permute-start(f32[3,4,16,128]{3,2,1,0:T(8,128)} %broadcast_in_dim.71), channel_id=1, source_target_pairs={{15,0},{0,1},{1,2},{2,3},{3,4},{4,5},{5,6},{6,7},{7,8},{8,9},{9,10... | collective-permute-start | bytes 294920 | tf_op jit(solution)/shard_map/ppermute | solution.py:19
  42.2 14.1 %collective-permute-start.12 = (f32[1,4,16,128]{3,2,0,1:T(8,128)S(1)}, f32[1,4,16,128]{3,2,0,1:T(8,128)S(1)}, u32[]{:S(2)}, u32[]{:S(2)}) collective-permute-start(f32[1,4,16,128]{3,2,0,1:T(8,128)S(1)} %get-tuple-element.757), channel_id=1, source_target_pairs={{15,0},{0,1},{1,2},{2,3},{3,4},{4,5},{5,6},{6,7},{7,8},{8,9},{9,10... | collective-permute-start | bytes 98312 | tf_op jit(solution)/shard_map/ppermute | solution.py:19
  42.3 15.2 %collective-permute-start.13 = (f32[1,4,16,128]{3,2,0,1:T(8,128)S(1)}, f32[1,4,16,128]{3,2,0,1:T(8,128)S(1)}, u32[]{:S(2)}, u32[]{:S(2)}) collective-permute-start(f32[1,4,16,128]{3,2,0,1:T(8,128)S(1)} %get-tuple-element.758), channel_id=1, source_target_pairs={{1,0},{2,1},{3,2},{4,3},{5,4},{6,5},{7,6},{8,7},{9,8},{10,9},{11,1... | collective-permute-start | bytes 98312 | tf_op jit(solution)/shard_map/ppermute | solution.py:19
  65.4 11.0 %collective-permute-start.15 = (f32[1,4,16,128]{3,2,0,1:T(8,128)S(1)}, f32[1,4,16,128]{3,2,0,1:T(8,128)S(1)}, u32[]{:S(2)}, u32[]{:S(2)}) collective-permute-start(f32[1,4,16,128]{3,2,0,1:T(8,128)S(1)} %get-tuple-element.756), channel_id=1, source_target_pairs={{1,0},{2,1},{3,2},{4,3},{5,4},{6,5},{7,6},{8,7},{9,8},{10,9},{11,1... | collective-permute-start | bytes 98312 | tf_op jit(solution)/shard_map/ppermute | solution.py:19
  127.3 11.6 %collective-permute-start.1 = (f32[1,4,16,128]{3,2,1,0:T(8,128)S(1)}, f32[1,4,16,128]{3,2,1,0:T(8,128)S(1)}, u32[]{:S(2)}, u32[]{:S(2)}) collective-permute-start(f32[1,4,16,128]{3,2,1,0:T(8,128)S(1)} %get-tuple-element.1016), channel_id=1, source_target_pairs={{1,0},{2,1},{3,2},{4,3},{5,4},{6,5},{7,6},{8,7},{9,8},{10,9},{11,1... | collective-permute-start | bytes 98312 | tf_op jit(solution)/shard_map/while/body/eval_jaxpr/ppermute | solution.py:19
  144.9 10.4 %collective-permute-start.3 = (f32[1,4,16,128]{3,2,1,0:T(8,128)S(1)}, f32[1,4,16,128]{3,2,1,0:T(8,128)S(1)}, u32[]{:S(2)}, u32[]{:S(2)}) collective-permute-start(f32[1,4,16,128]{3,2,1,0:T(8,128)S(1)} %get-tuple-element.1026), channel_id=1, source_target_pairs={{1,0},{2,1},{3,2},{4,3},{5,4},{6,5},{7,6},{8,7},{9,8},{10,9},{11,1... | collective-permute-start | bytes 98312 | tf_op jit(solution)/shard_map/while/body/eval_jaxpr/ppermute | solution.py:19
  167.3 11.7 %collective-permute-start.1 = (f32[1,4,16,128]{3,2,1,0:T(8,128)S(1)}, f32[1,4,16,128]{3,2,1,0:T(8,128)S(1)}, u32[]{:S(2)}, u32[]{:S(2)}) collective-permute-start(f32[1,4,16,128]{3,2,1,0:T(8,128)S(1)} %get-tuple-element.1016), channel_id=1, source_target_pairs={{1,0},{2,1},{3,2},{4,3},{5,4},{6,5},{7,6},{8,7},{9,8},{10,9},{11,1... | collective-permute-start | bytes 98312 | tf_op jit(solution)/shard_map/while/body/eval_jaxpr/ppermute | solution.py:19
  184.9 10.4 %collective-permute-start.3 = (f32[1,4,16,128]{3,2,1,0:T(8,128)S(1)}, f32[1,4,16,128]{3,2,1,0:T(8,128)S(1)}, u32[]{:S(2)}, u32[]{:S(2)}) collective-permute-start(f32[1,4,16,128]{3,2,1,0:T(8,128)S(1)} %get-tuple-element.1026), channel_id=1, source_target_pairs={{1,0},{2,1},{3,2},{4,3},{5,4},{6,5},{7,6},{8,7},{9,8},{10,9},{11,1... | collective-permute-start | bytes 98312 | tf_op jit(solution)/shard_map/while/body/eval_jaxpr/ppermute | solution.py:19
  207.3 11.7 %collective-permute-start.1 = (f32[1,4,16,128]{3,2,1,0:T(8,128)S(1)}, f32[1,4,16,128]{3,2,1,0:T(8,128)S(1)}, u32[]{:S(2)}, u32[]{:S(2)}) collective-permute-start(f32[1,4,16,128]{3,2,1,0:T(8,128)S(1)} %get-tuple-element.1016), channel_id=1, source_target_pairs={{1,0},{2,1},{3,2},{4,3},{5,4},{6,5},{7,6},{8,7},{9,8},{10,9},{11,1... | collective-permute-start | bytes 98312 | tf_op jit(solution)/shard_map/while/body/eval_jaxpr/ppermute | solution.py:19
  225.0 10.4 %collective-permute-start.3 = (f32[1,4,16,128]{3,2,1,0:T(8,128)S(1)}, f32[1,4,16,128]{3,2,1,0:T(8,128)S(1)}, u32[]{:S(2)}, u32[]{:S(2)}) collective-permute-start(f32[1,4,16,128]{3,2,1,0:T(8,128)S(1)} %get-tuple-element.1026), channel_id=1, source_target_pairs={{1,0},{2,1},{3,2},{4,3},{5,4},{6,5},{7,6},{8,7},{9,8},{10,9},{11,1... | collective-permute-start | bytes 98312 | tf_op jit(solution)/shard_map/while/body/eval_jaxpr/ppermute | solution.py:19
  247.4 11.7 %collective-permute-start.1 = (f32[1,4,16,128]{3,2,1,0:T(8,128)S(1)}, f32[1,4,16,128]{3,2,1,0:T(8,128)S(1)}, u32[]{:S(2)}, u32[]{:S(2)}) collective-permute-start(f32[1,4,16,128]{3,2,1,0:T(8,128)S(1)} %get-tuple-element.1016), channel_id=1, source_target_pairs={{1,0},{2,1},{3,2},{4,3},{5,4},{6,5},{7,6},{8,7},{9,8},{10,9},{11,1... | collective-permute-start | bytes 98312 | tf_op jit(solution)/shard_map/while/body/eval_jaxpr/ppermute | solution.py:19
  287.5 11.7 %collective-permute-start.1 = (f32[1,4,16,128]{3,2,1,0:T(8,128)S(1)}, f32[1,4,16,128]{3,2,1,0:T(8,128)S(1)}, u32[]{:S(2)}, u32[]{:S(2)}) collective-permute-start(f32[1,4,16,128]{3,2,1,0:T(8,128)S(1)} %get-tuple-element.1016), channel_id=1, source_target_pairs={{1,0},{2,1},{3,2},{4,3},{5,4},{6,5},{7,6},{8,7},{9,8},{10,9},{11,1... | collective-permute-start | bytes 98312 | tf_op jit(solution)/shard_map/while/body/eval_jaxpr/ppermute | solution.py:19
  305.2 10.4 %collective-permute-start.3 = (f32[1,4,16,128]{3,2,1,0:T(8,128)S(1)}, f32[1,4,16,128]{3,2,1,0:T(8,128)S(1)}, u32[]{:S(2)}, u32[]{:S(2)}) collective-permute-start(f32[1,4,16,128]{3,2,1,0:T(8,128)S(1)} %get-tuple-element.1026), channel_id=1, source_target_pairs={{1,0},{2,1},{3,2},{4,3},{5,4},{6,5},{7,6},{8,7},{9,8},{10,9},{11,1... | collective-permute-start | bytes 98312 | tf_op jit(solution)/shard_map/while/body/eval_jaxpr/ppermute | solution.py:19
  327.6 11.7 %collective-permute-start.1 = (f32[1,4,16,128]{3,2,1,0:T(8,128)S(1)}, f32[1,4,16,128]{3,2,1,0:T(8,128)S(1)}, u32[]{:S(2)}, u32[]{:S(2)}) collective-permute-start(f32[1,4,16,128]{3,2,1,0:T(8,128)S(1)} %get-tuple-element.1016), channel_id=1, source_target_pairs={{1,0},{2,1},{3,2},{4,3},{5,4},{6,5},{7,6},{8,7},{9,8},{10,9},{11,1... | collective-permute-start | bytes 98312 | tf_op jit(solution)/shard_map/while/body/eval_jaxpr/ppermute | solution.py:19
  367.7 11.7 %collective-permute-start.1 = (f32[1,4,16,128]{3,2,1,0:T(8,128)S(1)}, f32[1,4,16,128]{3,2,1,0:T(8,128)S(1)}, u32[]{:S(2)}, u32[]{:S(2)}) collective-permute-start(f32[1,4,16,128]{3,2,1,0:T(8,128)S(1)} %get-tuple-element.1016), channel_id=1, source_target_pairs={{1,0},{2,1},{3,2},{4,3},{5,4},{6,5},{7,6},{8,7},{9,8},{10,9},{11,1... | collective-permute-start | bytes 98312 | tf_op jit(solution)/shard_map/while/body/eval_jaxpr/ppermute | solution.py:19
  385.3 10.4 %collective-permute-start.3 = (f32[1,4,16,128]{3,2,1,0:T(8,128)S(1)}, f32[1,4,16,128]{3,2,1,0:T(8,128)S(1)}, u32[]{:S(2)}, u32[]{:S(2)}) collective-permute-start(f32[1,4,16,128]{3,2,1,0:T(8,128)S(1)} %get-tuple-element.1026), channel_id=1, source_target_pairs={{1,0},{2,1},{3,2},{4,3},{5,4},{6,5},{7,6},{8,7},{9,8},{10,9},{11,1... | collective-permute-start | bytes 98312 | tf_op jit(solution)/shard_map/while/body/eval_jaxpr/ppermute | solution.py:19
  406.7 14.0 %collective-permute-start.16 = (f32[3,4,16,128]{3,2,0,1:T(8,128)}, f32[3,4,16,128]{3,2,0,1:T(8,128)}, u32[]{:S(2)}, u32[]{:S(2)}) collective-permute-start(f32[3,4,16,128]{3,2,0,1:T(8,128)} %get-tuple-element.749), channel_id=1, source_target_pairs={{15,0},{0,1},{1,2},{2,3},{3,4},{4,5},{5,6},{6,7},{7,8},{8,9},{9,10... | collective-permute-start | bytes 294920 | tf_op jit(solution)/shard_map/ppermute | solution.py:19
  406.8 17.4 %collective-permute-start.17 = (f32[3,4,16,128]{3,2,0,1:T(8,128)}, f32[3,4,16,128]{3,2,0,1:T(8,128)}, u32[]{:S(2)}, u32[]{:S(2)}) collective-permute-start(f32[3,4,16,128]{3,2,0,1:T(8,128)} %get-tuple-element.750), channel_id=1, source_target_pairs={{1,0},{2,1},{3,2},{4,3},{5,4},{6,5},{7,6},{8,7},{9,8},{10,9},{11,1... | collective-permute-start | bytes 294920 | tf_op jit(solution)/shard_map/ppermute | solution.py:19
  434.7 12.1 %collective-permute-start.18 = (f32[1,4,16,128]{3,2,0,1:T(8,128)S(1)}, f32[1,4,16,128]{3,2,0,1:T(8,128)S(1)}, u32[]{:S(2)}, u32[]{:S(2)}) collective-permute-start(f32[1,4,16,128]{3,2,0,1:T(8,128)S(1)} %get-tuple-element.753), channel_id=1, source_target_pairs={{15,0},{0,1},{1,2},{2,3},{3,4},{4,5},{5,6},{6,7},{7,8},{8,9},{9,10... | collective-permute-start | bytes 98312 | tf_op jit(solution)/shard_map/ppermute | solution.py:19
  434.7 13.2 %collective-permute-start.19 = (f32[1,4,16,128]{3,2,0,1:T(8,128)S(1)}, f32[1,4,16,128]{3,2,0,1:T(8,128)S(1)}, u32[]{:S(2)}, u32[]{:S(2)}) collective-permute-start(f32[1,4,16,128]{3,2,0,1:T(8,128)S(1)} %get-tuple-element.754), channel_id=1, source_target_pairs={{1,0},{2,1},{3,2},{4,3},{5,4},{6,5},{7,6},{8,7},{9,8},{10,9},{11,1... | collective-permute-start | bytes 98312 | tf_op jit(solution)/shard_map/ppermute | solution.py:19
  454.7 11.0 %collective-permute-start.21 = (f32[1,4,16,128]{3,2,0,1:T(8,128)S(1)}, f32[1,4,16,128]{3,2,0,1:T(8,128)S(1)}, u32[]{:S(2)}, u32[]{:S(2)}) collective-permute-start(f32[1,4,16,128]{3,2,0,1:T(8,128)S(1)} %get-tuple-element.752), channel_id=1, source_target_pairs={{1,0},{2,1},{3,2},{4,3},{5,4},{6,5},{7,6},{8,7},{9,8},{10,9},{11,1... | collective-permute-start | bytes 98312 | tf_op jit(solution)/shard_map/ppermute | solution.py:19
  516.5 11.6 %collective-permute-start.6 = (f32[1,4,16,128]{3,2,1,0:T(8,128)S(1)}, f32[1,4,16,128]{3,2,1,0:T(8,128)S(1)}, u32[]{:S(2)}, u32[]{:S(2)}) collective-permute-start(f32[1,4,16,128]{3,2,1,0:T(8,128)S(1)} %get-tuple-element.1053), channel_id=1, source_target_pairs={{1,0},{2,1},{3,2},{4,3},{5,4},{6,5},{7,6},{8,7},{9,8},{10,9},{11,1... | collective-permute-start | bytes 98312 | tf_op jit(solution)/shard_map/while/body/eval_jaxpr/ppermute | solution.py:19
  534.1 10.4 %collective-permute-start.8 = (f32[1,4,16,128]{3,2,1,0:T(8,128)S(1)}, f32[1,4,16,128]{3,2,1,0:T(8,128)S(1)}, u32[]{:S(2)}, u32[]{:S(2)}) collective-permute-start(f32[1,4,16,128]{3,2,1,0:T(8,128)S(1)} %get-tuple-element.1063), channel_id=1, source_target_pairs={{1,0},{2,1},{3,2},{4,3},{5,4},{6,5},{7,6},{8,7},{9,8},{10,9},{11,1... | collective-permute-start | bytes 98312 | tf_op jit(solution)/shard_map/while/body/eval_jaxpr/ppermute | solution.py:19
  556.5 11.7 %collective-permute-start.6 = (f32[1,4,16,128]{3,2,1,0:T(8,128)S(1)}, f32[1,4,16,128]{3,2,1,0:T(8,128)S(1)}, u32[]{:S(2)}, u32[]{:S(2)}) collective-permute-start(f32[1,4,16,128]{3,2,1,0:T(8,128)S(1)} %get-tuple-element.1053), channel_id=1, source_target_pairs={{1,0},{2,1},{3,2},{4,3},{5,4},{6,5},{7,6},{8,7},{9,8},{10,9},{11,1... | collective-permute-start | bytes 98312 | tf_op jit(solution)/shard_map/while/body/eval_jaxpr/ppermute | solution.py:19
  596.6 11.7 %collective-permute-start.6 = (f32[1,4,16,128]{3,2,1,0:T(8,128)S(1)}, f32[1,4,16,128]{3,2,1,0:T(8,128)S(1)}, u32[]{:S(2)}, u32[]{:S(2)}) collective-permute-start(f32[1,4,16,128]{3,2,1,0:T(8,128)S(1)} %get-tuple-element.1053), channel_id=1, source_target_pairs={{1,0},{2,1},{3,2},{4,3},{5,4},{6,5},{7,6},{8,7},{9,8},{10,9},{11,1... | collective-permute-start | bytes 98312 | tf_op jit(solution)/shard_map/while/body/eval_jaxpr/ppermute | solution.py:19
  614.3 10.4 %collective-permute-start.8 = (f32[1,4,16,128]{3,2,1,0:T(8,128)S(1)}, f32[1,4,16,128]{3,2,1,0:T(8,128)S(1)}, u32[]{:S(2)}, u32[]{:S(2)}) collective-permute-start(f32[1,4,16,128]{3,2,1,0:T(8,128)S(1)} %get-tuple-element.1063), channel_id=1, source_target_pairs={{1,0},{2,1},{3,2},{4,3},{5,4},{6,5},{7,6},{8,7},{9,8},{10,9},{11,1... | collective-permute-start | bytes 98312 | tf_op jit(solution)/shard_map/while/body/eval_jaxpr/ppermute | solution.py:19
  636.7 11.7 %collective-permute-start.6 = (f32[1,4,16,128]{3,2,1,0:T(8,128)S(1)}, f32[1,4,16,128]{3,2,1,0:T(8,128)S(1)}, u32[]{:S(2)}, u32[]{:S(2)}) collective-permute-start(f32[1,4,16,128]{3,2,1,0:T(8,128)S(1)} %get-tuple-element.1053), channel_id=1, source_target_pairs={{1,0},{2,1},{3,2},{4,3},{5,4},{6,5},{7,6},{8,7},{9,8},{10,9},{11,1... | collective-permute-start | bytes 98312 | tf_op jit(solution)/shard_map/while/body/eval_jaxpr/ppermute | solution.py:19
  676.8 11.7 %collective-permute-start.6 = (f32[1,4,16,128]{3,2,1,0:T(8,128)S(1)}, f32[1,4,16,128]{3,2,1,0:T(8,128)S(1)}, u32[]{:S(2)}, u32[]{:S(2)}) collective-permute-start(f32[1,4,16,128]{3,2,1,0:T(8,128)S(1)} %get-tuple-element.1053), channel_id=1, source_target_pairs={{1,0},{2,1},{3,2},{4,3},{5,4},{6,5},{7,6},{8,7},{9,8},{10,9},{11,1... | collective-permute-start | bytes 98312 | tf_op jit(solution)/shard_map/while/body/eval_jaxpr/ppermute | solution.py:19
  716.9 11.7 %collective-permute-start.6 = (f32[1,4,16,128]{3,2,1,0:T(8,128)S(1)}, f32[1,4,16,128]{3,2,1,0:T(8,128)S(1)}, u32[]{:S(2)}, u32[]{:S(2)}) collective-permute-start(f32[1,4,16,128]{3,2,1,0:T(8,128)S(1)} %get-tuple-element.1053), channel_id=1, source_target_pairs={{1,0},{2,1},{3,2},{4,3},{5,4},{6,5},{7,6},{8,7},{9,8},{10,9},{11,1... | collective-permute-start | bytes 98312 | tf_op jit(solution)/shard_map/while/body/eval_jaxpr/ppermute | solution.py:19
  734.5 10.4 %collective-permute-start.8 = (f32[1,4,16,128]{3,2,1,0:T(8,128)S(1)}, f32[1,4,16,128]{3,2,1,0:T(8,128)S(1)}, u32[]{:S(2)}, u32[]{:S(2)}) collective-permute-start(f32[1,4,16,128]{3,2,1,0:T(8,128)S(1)} %get-tuple-element.1063), channel_id=1, source_target_pairs={{1,0},{2,1},{3,2},{4,3},{5,4},{6,5},{7,6},{8,7},{9,8},{10,9},{11,1... | collective-permute-start | bytes 98312 | tf_op jit(solution)/shard_map/while/body/eval_jaxpr/ppermute | solution.py:19
  757.0 11.7 %collective-permute-start.6 = (f32[1,4,16,128]{3,2,1,0:T(8,128)S(1)}, f32[1,4,16,128]{3,2,1,0:T(8,128)S(1)}, u32[]{:S(2)}, u32[]{:S(2)}) collective-permute-start(f32[1,4,16,128]{3,2,1,0:T(8,128)S(1)} %get-tuple-element.1053), channel_id=1, source_target_pairs={{1,0},{2,1},{3,2},{4,3},{5,4},{6,5},{7,6},{8,7},{9,8},{10,9},{11,1... | collective-permute-start | bytes 98312 | tf_op jit(solution)/shard_map/while/body/eval_jaxpr/ppermute | solution.py:19
  (154 other events, 1084.4 us)
where the time goes:
time: 800 us; the launch traced here: 789 us
  local copies, waits for them, and re-layouts  411 us (51%)
  starting transfers between devices  163 us (20%)
  waiting for transfers between devices  110 us (14%)
  matrix products  66 us (8%)
  other arithmetic  23.2 us (3%)
  loops' own time  11.7 us (1%)
    gather x456, local copies, waits for them, and re-layouts, apply_operator(): outside = jnp.take(source, flat_index[face], axis=3)  201 us
    ppermute x76, starting transfers between devices, from_behind(): return lax.ppermute(block, axis, route)  124 us
    ppermute x16, waiting for transfers between devices, from_behind_2(): lax.ppermute(value, axis, [(source, source + steps) for source in range(i...  106 us
    gather x230, local copies, waits for them, and re-layouts, apply_operator(): inside = jnp.take(field, inside_lists[face], axis=2)  93 us
    dot_general x380, matrix products, node_product(): jnp.einsum('mn,kne->kme', matrix, value, precision=lax.Precision.HIGHEST)  66 us
    gather x156, local copies, waits for them, and re-layouts, apply_operator(): source = jnp.take(field, outside_lists[face], axis=2)  47.5 us
    ppermute x16, starting transfers between devices, from_behind_2(): lax.ppermute(value, axis, [(source, source + steps) for source in range(i...  39.8 us
    another operation x216, local copies, waits for them, and re-layouts, apply_operator(): outside = jnp.take(source, flat_index[face], axis=3)  34.2 us
  transfers between devices with their start and end apart: 92, of which 32 were waited for; matrix products, arithmetic and copies ran while one was open for 38% of the time, Pallas kernels for 0%

commit v1 on v0

v1 whole, which is shorter than its diff:
```python
import functools

import jax
import jax.numpy as jnp
import numpy as np
from jax import lax
from jax.experimental import pallas as pl
from jax.experimental.pallas import tpu as pltpu
from jax.sharding import PartitionSpec as P

ORDER = 4
NODES = 64
ITERS = 2
FIELDS = 4
SLICES = 8
LAYERS = 16
CELLS = 128
ROWS = FIELDS * NODES
PART = ROWS + 8
DEGREE = 22
BASE_STEP = 0.015

OFFSETS = (
    ((0, 1), ((2, 0), (2, 1))),
    ((1, 1), ((1, 0), (1, 1))),
    ((3, 1), ((3, 0), (3, 1))),
    ((1, 0), ((0, 0), (0, 0))),
    ((3, 0), ((0, 0), (0, 0))),
    ((2, 0), ((0, 0), (0, 0))),
    ((2, 1), ((0, 0), (0, 1))),
)


def modal_tables():
    points = np.array([-1.0, -1.0 / np.sqrt(5.0), 1.0 / np.sqrt(5.0), 1.0])
    to_nodes = np.polynomial.legendre.legvander(points, ORDER - 1)
    to_modes = np.linalg.inv(to_nodes)
    cube = lambda m: np.kron(np.kron(m, m), m).astype(np.float32)
    return cube(to_modes), cube(to_nodes)


def route(move):
    pairs = []
    for x in range(4):
        for high in range(2):
            for y in range(4):
                for low in range(2):
                    for core in range(2):
                        to_x, to_high, to_y, to_low, to_core = move(x, high, y, low, core)
                        source = (x * 2 + high) * 16 + y * 4 + low * 2 + core
                        target = (to_x % 4 * 2 + to_high % 2) * 16 + to_y % 4 * 4 + to_low % 2 * 2 + to_core % 2
                        pairs.append((source, target))
    return pairs


def prepare_kernel(step_ref, state_ref, near_ref, table_ref, out_ref):
    table = table_ref[...]
    for field in range(FIELDS):
        rows = pl.ds(field * NODES, NODES)
        out_ref[rows, :] = jnp.dot(
            table, state_ref[rows, :], precision=lax.Precision.HIGHEST, preferred_element_type=jnp.float32
        )
    near = near_ref[...].astype(jnp.float32)
    lane = lax.broadcasted_iota(jnp.int32, (2, CELLS), 1)
    count = jnp.where(lane == lax.axis_index("tm"), step_ref[0], 0).astype(jnp.float32)
    out_ref[pl.ds(ROWS, 8), :] = jnp.concatenate([near, count], axis=0)


def directional(p, u, fetch):
    o_u = u[1] + u[3]
    o_p = p[1] + p[3]
    m = (u[0] + u[2]) + o_p
    n = (p[0] + p[2]) + o_u
    x, y = m - n, m + n
    x_near, y_near = fetch(x, y)
    d_x = x_near - x
    d_y = y_near - y
    p_0 = 0.25 * (d_y - d_x)
    u_0 = 0.25 * (d_x + d_y)
    t = u_0 + o_p
    w = p_0 + o_u
    rate_p = [p_0, -3.0 * (t + u[2]), 5.0 * (p_0 + u[1]), -3.0 * t]
    rate_u = [u_0, -3.0 * (w + p[2]), 5.0 * (u_0 + p[1]), -3.0 * w]
    return rate_p, rate_u


def lanes(value, index):
    return jnp.take_along_axis(value, index, axis=1, mode="promise_in_bounds")


def row(field, a, b, c, v):
    return (field * NODES + a * 16 + b * 4 + c) * LAYERS + v * 8


def apply_operator(src, dst, index_ref):
    get = lambda r: src[pl.ds(r, 8), :]

    def put(r, value):
        dst[pl.ds(r, 8), :] = value

    index = lambda face, v: index_ref[pl.ds(face * LAYERS + v * 8, 8), :]
    four = range(ORDER)
    for b in four:
        for c in four:
            p = [[get(row(0, a, b, c, v)) for a in four] for v in range(2)]
            u = [[get(row(1, a, b, c, v)) for a in four] for v in range(2)]
            ends = []
            for v in range(2):
                o_u = u[v][1] + u[v][3]
                o_p = p[v][1] + p[v][3]
                m = (u[v][0] + u[v][2]) + o_p
                n = (p[v][0] + p[v][2]) + o_u
                ends.append((m - n, m + n))
            x_near = [lanes(ends[1][0], index(1, 0)), lanes(pltpu.roll(ends[0][0], 7, 0), index(1, 1))]
            y_near = [lanes(pltpu.roll(ends[1][1], 1, 0), index(0, 0)), lanes(ends[0][1], index(0, 1))]
            for v in range(2):
                rate_p, rate_u = directional(p[v], u[v], lambda x, y: (x_near[v], y_near[v]))
                for a in four:
                    put(row(0, a, b, c, v), rate_p[a])
                    put(row(1, a, b, c, v), rate_u[a])
    for v in range(2):
        for a in four:
            p = [[get(row(0, a, b, c, v)) for c in four] for b in four]
            rate = [[dst[pl.ds(row(0, a, b, c, v), 8), :] for c in four] for b in four]
            for c in four:
                u = [get(row(2, a, b, c, v)) for b in four]
                fetch = lambda x, y: (lanes(x, index(3, v)), lanes(y, index(2, v)))
                rate_p, rate_u = directional([p[b][c] for b in four], u, fetch)
                for b in four:
                    rate[b][c] = rate[b][c] + rate_p[b]
                    put(row(2, a, b, c, v), rate_u[b])
            for b in four:
                u = [get(row(3, a, b, c, v)) for c in four]
                fetch = lambda x, y: (lanes(x, index(5, v)), lanes(y, index(4, v)))
                rate_p, rate_u = directional(p[b], u, fetch)
                for c in four:
                    put(row(0, a, b, c, v), rate[b][c] + rate_p[c])
                    put(row(3, a, b, c, v), rate_u[c])


def coefficients(counts):
    rows = lax.broadcasted_iota(jnp.int32, (SLICES, CELLS), 0)
    lane = lax.broadcasted_iota(jnp.int32, (SLICES, CELLS), 1)
    wide = jnp.broadcast_to(counts, (SLICES, CELLS))
    h = jnp.sum(jnp.where(rows == lane, wide, 0.0), axis=1, keepdims=True) * BASE_STEP
    h = jnp.broadcast_to(h, (SLICES, CELLS))
    image = lambda value: pltpu.roll(value, 1, 1)
    initial = jnp.where(lane == 0, 1.0, 0.0)
    spread = lambda value, n: jnp.broadcast_to(value[n : n + 1], (SLICES, CELLS))
    u_0 = u_1 = u_2 = initial
    for _ in range(ITERS):
        old_0, old_1, old_2 = image(u_0), image(u_1), image(u_2)
        first = u_0 + h * (5.0 / 24.0 * old_0 + 1.0 / 3.0 * old_1 - 1.0 / 24.0 * old_2)
        image_first = image(first)
        second = (
            first
            + h * (image_first - old_1)
            + h * (-1.0 / 24.0 * old_0 + 1.0 / 3.0 * old_1 + 5.0 / 24.0 * old_2)
        )
        image_second = image(second)
        correction = h * (2.0 / 3.0 * image_first - 1.0 / 3.0 * old_0 - 1.0 / 3.0 * image_second)
        carried = h * (0.5 * image_second - 0.5 * old_0) + correction
        begin = initial
        begins = initial
        finishes = initial
        for n in range(SLICES):
            h_n = spread(h, n)
            begin_image = image(begin)
            middle_image = image(begin + h_n * begin_image + spread(carried, n))
            finish = begin + 0.5 * h_n * (begin_image + middle_image) + spread(correction, n)
            begins = jnp.where(rows == n, begin, begins)
            finishes = jnp.where(rows == n, finish, finishes)
            begin = finish
        u_1 = first + 0.5 * ((begins - u_0) + (finishes - second))
        u_0, u_2 = begins, finishes
    return u_0, u_1, u_2


def advance_kernel(*refs):
    parts = refs[:LAYERS]
    table_ref, out_ref, one, two, index_ref, saved, coef_ref, spread_ref, sum_ref = refs[LAYERS:]
    space = lax.axis_index("space")
    core = space % 2
    chip = space // 2
    low = chip % 2
    high = chip // 2
    place = lambda layer: (layer % 2) * 8 + layer // 2
    counts = jnp.zeros((1, CELLS), jnp.float32)
    for k, part in enumerate(parts):
        offset = ((0, 0),) + tuple(o for o, _ in OFFSETS)
        step_y, step_z = offset[k % 8]
        from_y = (high + 4 - step_y) % 4
        from_z = (low + step_z) % 2
        layer = from_y * 4 + from_z * 2 + (core if k < 8 else 1 - core)
        base = place(layer)
        for m in range(ROWS // 8):
            one[pl.ds(m * 8 * LAYERS + base, 8, stride=LAYERS), :] = part[pl.ds(m * 8, 8), :]
        tail = part[pl.ds(ROWS, 8), :]
        for face in range(6):
            index_ref[pl.ds(face * LAYERS + base, 1), :] = tail[face : face + 1].astype(jnp.int32)
        counts = jnp.maximum(counts, tail[6:7])

    polynomials = coefficients(counts)
    for m in range(3):
        coef_ref[pl.ds(m * 8, 8), :] = polynomials[m]
    own_slice = lax.axis_index("tm")
    for m in range(3):
        mine = jnp.broadcast_to(coef_ref[pl.ds(m * 8 + own_slice, 1), :], (8, CELLS))
        for k in range(DEGREE + 1):
            spread_ref[pl.ds((k * 3 + m) * 8, 8), :] = jnp.broadcast_to(mine[:, k : k + 1], (8, CELLS))

    own = place(space)

    def keep(source, k):
        for m in range(ROWS // 8):
            saved[pl.ds(k * ROWS + m * 8, 8), :] = source[pl.ds(m * 8 * LAYERS + own, 8, stride=LAYERS), :]

    keep(one, 0)

    def advance(turn, carry):
        apply_operator(one, two, index_ref)
        keep(two, 2 * turn + 1)
        apply_operator(two, one, index_ref)
        keep(one, 2 * turn + 2)
        return carry

    lax.fori_loop(0, DEGREE // 2, advance, 0)

    group = 16

    def combine(g, carry):
        total = [[None] * group for _ in range(3)]
        for k in range(DEGREE + 1):
            value = [saved[pl.ds(k * ROWS + (g * group + i) * 8, 8), :] for i in range(group)]
            for m in range(3):
                factor = spread_ref[pl.ds((k * 3 + m) * 8, 8), :]
                for i in range(group):
                    term = factor * value[i]
                    total[m][i] = term if total[m][i] is None else total[m][i] + term
        for m in range(3):
            for i in range(group):
                sum_ref[pl.ds(m * ROWS + (g * group + i) * 8, 8), :] = total[m][i]
        return carry

    lax.fori_loop(0, ROWS // 8 // group, combine, 0)
    table = table_ref[...]
    for m in range(3 * FIELDS):
        rows = pl.ds(m * NODES, NODES)
        out_ref[rows, :] = jnp.dot(
            table, sum_ref[rows, :], precision=lax.Precision.HIGHEST, preferred_element_type=jnp.float32
        )


def shards(initial, neighbours, step_counts):
    to_modes, to_nodes = modal_tables()
    state = initial.reshape(ROWS, CELLS)
    near = neighbours.reshape(6, CELLS)
    whole = lambda: pl.BlockSpec(memory_space=pltpu.VMEM)
    part = pl.pallas_call(
        prepare_kernel,
        out_shape=jax.ShapeDtypeStruct((PART, CELLS), jnp.float32),
        in_specs=[pl.BlockSpec(memory_space=pltpu.SMEM), whole(), whole(), whole()],
        out_specs=whole(),
    )(step_counts, state, near, jnp.asarray(to_modes))

    axes = ("tm", "space")
    parts = [part]
    for (step_y, step_z), skew in OFFSETS:

        def move(x, high, y, low, core):
            return (x + skew[core][0], high + skew[core][1], y + step_y, low + step_z, core)

        parts.append(lax.ppermute(part, axes, route(move)))
    swap = route(lambda x, high, y, low, core: (x, high, y, low, core + 1))
    parts += [lax.ppermute(value, axes, swap) for value in parts]

    result = pl.pallas_call(
        advance_kernel,
        out_shape=jax.ShapeDtypeStruct((3 * ROWS, CELLS), jnp.float32),
        in_specs=[whole() for _ in range(LAYERS + 1)],
        out_specs=whole(),
        scratch_shapes=[
            pltpu.VMEM((ROWS * LAYERS, CELLS), jnp.float32),
            pltpu.VMEM((ROWS * LAYERS, CELLS), jnp.float32),
            pltpu.VMEM((6 * LAYERS, CELLS), jnp.int32),
            pltpu.VMEM(((DEGREE + 1) * ROWS, CELLS), jnp.float32),
            pltpu.VMEM((24, CELLS), jnp.float32),
            pltpu.VMEM(((DEGREE + 1) * 3 * 8, CELLS), jnp.float32),
            pltpu.VMEM((3 * ROWS, CELLS), jnp.float32),
        ],
        compiler_params=pltpu.CompilerParams(vmem_limit_bytes=32 * 1024 * 1024),
    )(*parts, jnp.asarray(to_nodes))
    return result.reshape(1, 3, FIELDS, NODES, 1, CELLS)


def solution(mesh):
    placed = (P(None, None, "space", None), P(None, "space", None), P("tm"))
    return jax.shard_map(
        shards,
        mesh=mesh,
        in_specs=placed,
        out_specs=P("tm", None, None, None, "space", None),
        check_vma=False,
    )
```

time: 800 us -> 55.9 us (0.07)
  the two profiles are of different devices: /device:TPU:6 before, /device:TPU:1 now
where the time goes in v1:
time: 55.9 us; the launch traced here: 55.7 us
  starting transfers between devices  23.2 us (42%)
  Pallas kernels  22.9 us (41%)
  waiting for transfers between devices  6.82 us (12%)
  local copies, waits for them, and re-layouts  2.19 us (4%)
  between operations  0.67 us (1%)
    pallas_call x1, Pallas kernels, shards(): pl.pallas_call(advance_kernel, out_shape=jax.ShapeDtypeStruct((3 * ROWS,...  21.1 us
    ppermute x7, starting transfers between devices, shards(): parts.append(lax.ppermute(part, axes, route(move)))  16.8 us
    ppermute x8, starting transfers between devices, shards(): parts += [lax.ppermute(value, axes, swap) for value in parts]  6.31 us
    ppermute x7, waiting for transfers between devices, shards(): parts.append(lax.ppermute(part, axes, route(move)))  5.54 us
    unnamed x5, local copies, waits for them, and re-layouts  2.19 us
    pallas_call x1, Pallas kernels, shards(): pl.pallas_call(prepare_kernel, out_shape=jax.ShapeDtypeStruct((PART, CELL...  1.82 us
    ppermute x8, waiting for transfers between devices, shards(): parts += [lax.ppermute(value, axes, swap) for value in parts]  1.28 us
  transfers between devices with their start and end apart: 15, of which 6 were waited for; matrix products, arithmetic and copies ran while one was open for 0% of the time, Pallas kernels for 0%

profile of v1, /device:TPU:1, one launch (start us, length us, event | category | flops | bytes accessed | tf_op | source)
XLA Modules:
  0.0 55.7 jit_solution(4040108152547435513)
XLA Ops:
  0.7 1.3 %copy.9 = s32[6,1,128]{2,0,1:T(8,128)} copy(s32[6,1,128]{2,1,0:T(1,128)} %param.6) | data formatting | bytes 6144
  1.9 1.8 %shard_map.55.refs_0_ = f32[264,128]{1,0:T(8,128)} custom-call(s32[1]{0:T(128)S(6)} %copy.10.step_ref, f32[256,128]{1,0:T(8,128)} %bitcast.7, s32[6,128]{1,0:T(8,128)} %bitcast.8, f32[64,64]{1,0:T(8,128)} %constant.4.clone.table_ref), custom_call_target="tpu_custom_call" | custom-call | tf_op jit(solution)/shard_map/pallas_call | solution.py:259
  3.8 1.4 %collective-permute-start.7 = (f32[264,128]{1,0:T(8,128)}, f32[264,128]{1,0:T(8,128)S(1)}, u32[]{:S(2)}, u32[]{:S(2)}) collective-permute-start(f32[264,128]{1,0:T(8,128)} %shard_map.55.refs_0_), channel_id=1, source_target_pairs={{0,1},{1,0},{2,3},{3,2},{4,5},{5,4},{6,7},{7,6},{8,9},{9,8},{10,11... | collective-permute-start | bytes 405512 | tf_op jit(solution)/shard_map/ppermute | solution.py:275
  5.2 6.5 %collective-permute-start.6 = (f32[264,128]{1,0:T(8,128)}, f32[264,128]{1,0:T(8,128)S(1)}, u32[]{:S(2)}, u32[]{:S(2)}) collective-permute-start(f32[264,128]{1,0:T(8,128)} %shard_map.55.refs_0_), channel_id=1, source_target_pairs={{0,10},{1,27},{2,8},{3,25},{4,14},{5,31},{6,12},{7,29},{8,2},{9,19... | collective-permute-start | bytes 405512 | tf_op jit(solution)/shard_map/ppermute | solution.py:273
  11.6 0.1 collective-permute-start.5
  11.7 2.7 %collective-permute-start.4 = (f32[264,128]{1,0:T(8,128)}, f32[264,128]{1,0:T(8,128)S(1)}, u32[]{:S(2)}, u32[]{:S(2)}) collective-permute-start(f32[264,128]{1,0:T(8,128)} %shard_map.55.refs_0_), channel_id=1, source_target_pairs={{0,12},{1,13},{2,14},{3,15},{4,0},{5,1},{6,2},{7,3},{8,4},{9,5},{1... | collective-permute-start | bytes 405512 | tf_op jit(solution)/shard_map/ppermute | solution.py:273
  14.4 0.0 collective-permute-start.3
  14.4 0.0 collective-permute-done.7.refs_8_
  14.4 3.5 %collective-permute-start.2 = (f32[264,128]{1,0:T(8,128)}, f32[264,128]{1,0:T(8,128)S(1)}, u32[]{:S(2)}, u32[]{:S(2)}) collective-permute-start(f32[264,128]{1,0:T(8,128)} %shard_map.55.refs_0_), channel_id=1, source_target_pairs={{0,110},{1,127},{2,108},{3,125},{4,98},{5,115},{6,96},{7,113},{8,1... | collective-permute-start | bytes 405512 | tf_op jit(solution)/shard_map/ppermute | solution.py:273
  17.9 0.0 collective-permute-done.6.refs_7_
  18.0 1.7 %collective-permute-start.1 = (f32[264,128]{1,0:T(8,128)}, f32[264,128]{1,0:T(8,128)S(1)}, u32[]{:S(2)}, u32[]{:S(2)}) collective-permute-start(f32[264,128]{1,0:T(8,128)} %shard_map.55.refs_0_), channel_id=1, source_target_pairs={{0,38},{1,55},{2,36},{3,53},{4,42},{5,59},{6,40},{7,57},{8,46},{9,... | collective-permute-start | bytes 405512 | tf_op jit(solution)/shard_map/ppermute | solution.py:273
  19.6 0.0 collective-permute-done.5.refs_6_
  19.6 2.4 %collective-permute-start = (f32[264,128]{1,0:T(8,128)}, f32[264,128]{1,0:T(8,128)S(1)}, u32[]{:S(2)}, u32[]{:S(2)}) collective-permute-start(f32[264,128]{1,0:T(8,128)} %shard_map.55.refs_0_), channel_id=1, source_target_pairs={{0,66},{1,83},{2,64},{3,81},{4,70},{5,87},{6,68},{7,85},{8,74},{9,... | collective-permute-start | bytes 405512 | tf_op jit(solution)/shard_map/ppermute | solution.py:273
  22.0 1.1 %collective-permute-done.4.refs_5_ = f32[264,128]{1,0:T(8,128)S(1)} collective-permute-done((f32[264,128]{1,0:T(8,128)}, f32[264,128]{1,0:T(8,128)S(1)}, u32[]{:S(2)}, u32[]{:S(2)}) %collective-permute-start.4) | collective-permute-done | bytes 135200 | tf_op jit(solution)/shard_map/ppermute | solution.py:273
  23.1 0.0 collective-permute-start.14
  23.1 0.0 collective-permute-done.3.refs_4_
  23.1 0.5 collective-permute-start.13
  23.6 0.0 collective-permute-done.2.refs_3_
  23.7 0.1 collective-permute-start.12
  23.7 4.4 %collective-permute-done.1.refs_2_ = f32[264,128]{1,0:T(8,128)S(1)} collective-permute-done((f32[264,128]{1,0:T(8,128)}, f32[264,128]{1,0:T(8,128)S(1)}, u32[]{:S(2)}, u32[]{:S(2)}) %collective-permute-start.1) | collective-permute-done | bytes 135200 | tf_op jit(solution)/shard_map/ppermute | solution.py:273
  28.2 3.7 %collective-permute-start.11 = (f32[264,128]{1,0:T(8,128)S(1)}, f32[264,128]{1,0:T(8,128)S(1)}, u32[]{:S(2)}, u32[]{:S(2)}) collective-permute-start(f32[264,128]{1,0:T(8,128)S(1)} %collective-permute-done.3.refs_4_), channel_id=1, source_target_pairs={{0,1},{1,0},{2,3},{3,2},{4,5},{5,4},{6,7},{7,6},{8,9},{9,8},{10,11... | collective-permute-start | bytes 405512 | tf_op jit(solution)/shard_map/ppermute | solution.py:275
  31.9 0.0 collective-permute-done.refs_1_
  31.9 0.0 collective-permute-start.10
  31.9 0.0 collective-permute-done.14.refs_15_
  31.9 0.5 collective-permute-start.9
  32.4 0.1 collective-permute-start.8
  32.5 0.4 collective-permute-done.11.refs_12_
  32.9 0.4 collective-permute-done.10.refs_11_
  33.2 0.2 collective-permute-done.9.refs_10_
  33.4 0.3 collective-permute-done.8.refs_9_
  33.8 0.9 %copy-done = f32[264,128]{1,0:T(8,128)S(1)} copy-done((f32[264,128]{1,0:T(8,128)S(1)}, f32[264,128]{1,0:T(8,128)}, u32[]{:S(2)}) %copy-start) | copy-done | bytes 135192
  34.7 21.1 %shard_map.56 = f32[768,128]{1,0:T(8,128)} custom-call(f32[264,128]{1,0:T(8,128)S(1)} %copy-done, f32[264,128]{1,0:T(8,128)S(1)} %collective-permute-done.refs_1_, f32[264,128]{1,0:T(8,128)S(1)} %collective-permute-done.1.refs_2_, f32[264,128]{1,0:T(8,128)S(1)} %collective-permute-done.2.refs_3_, f32[264,128]{1,0:T(8,128)S(1)} %collective-permute-done.3.refs_4_, ...), custom_call_target="tpu_custom_call" | custom-call | tf_op jit(solution)/shard_map/pallas_call | solution.py:277
  (5 shorter events, 0.0 us)
Async XLA Ops:
  1.9 31.8 %copy-start.1 = (f32[64,64]{1,0:T(8,128)S(1)}, f32[64,64]{1,0:T(8,128)}, u32[]{:S(2)}) copy-start(f32[64,64]{1,0:T(8,128)} %constant.5.clone.refs_16_) | copy-start | bytes 49156
  3.8 10.7 %collective-permute-start.7 = (f32[264,128]{1,0:T(8,128)}, f32[264,128]{1,0:T(8,128)S(1)}, u32[]{:S(2)}, u32[]{:S(2)}) collective-permute-start(f32[264,128]{1,0:T(8,128)} %shard_map.55.refs_0_), channel_id=1, source_target_pairs={{0,1},{1,0},{2,3},{3,2},{4,5},{5,4},{6,7},{7,6},{8,9},{9,8},{10,11... | collective-permute-start | bytes 405512 | tf_op jit(solution)/shard_map/ppermute | solution.py:275
  5.2 12.8 %collective-permute-start.6 = (f32[264,128]{1,0:T(8,128)}, f32[264,128]{1,0:T(8,128)S(1)}, u32[]{:S(2)}, u32[]{:S(2)}) collective-permute-start(f32[264,128]{1,0:T(8,128)} %shard_map.55.refs_0_), channel_id=1, source_target_pairs={{0,10},{1,27},{2,8},{3,25},{4,14},{5,31},{6,12},{7,29},{8,2},{9,19... | collective-permute-start | bytes 405512 | tf_op jit(solution)/shard_map/ppermute | solution.py:273
  11.6 8.0 %collective-permute-start.5 = (f32[264,128]{1,0:T(8,128)}, f32[264,128]{1,0:T(8,128)S(1)}, u32[]{:S(2)}, u32[]{:S(2)}) collective-permute-start(f32[264,128]{1,0:T(8,128)} %shard_map.55.refs_0_), channel_id=1, source_target_pairs={{0,8},{1,9},{2,10},{3,11},{4,12},{5,13},{6,14},{7,15},{8,0},{9,1},... | collective-permute-start | bytes 405512 | tf_op jit(solution)/shard_map/ppermute | solution.py:273
  11.7 11.4 %collective-permute-start.4 = (f32[264,128]{1,0:T(8,128)}, f32[264,128]{1,0:T(8,128)S(1)}, u32[]{:S(2)}, u32[]{:S(2)}) collective-permute-start(f32[264,128]{1,0:T(8,128)} %shard_map.55.refs_0_), channel_id=1, source_target_pairs={{0,12},{1,13},{2,14},{3,15},{4,0},{5,1},{6,2},{7,3},{8,4},{9,5},{1... | collective-permute-start | bytes 405512 | tf_op jit(solution)/shard_map/ppermute | solution.py:273
  14.4 8.7 %collective-permute-start.3 = (f32[264,128]{1,0:T(8,128)}, f32[264,128]{1,0:T(8,128)S(1)}, u32[]{:S(2)}, u32[]{:S(2)}) collective-permute-start(f32[264,128]{1,0:T(8,128)} %shard_map.55.refs_0_), channel_id=1, source_target_pairs={{0,4},{1,5},{2,6},{3,7},{4,8},{5,9},{6,10},{7,11},{8,12},{9,13},{1... | collective-permute-start | bytes 405512 | tf_op jit(solution)/shard_map/ppermute | solution.py:273
  14.4 9.2 %collective-permute-start.2 = (f32[264,128]{1,0:T(8,128)}, f32[264,128]{1,0:T(8,128)S(1)}, u32[]{:S(2)}, u32[]{:S(2)}) collective-permute-start(f32[264,128]{1,0:T(8,128)} %shard_map.55.refs_0_), channel_id=1, source_target_pairs={{0,110},{1,127},{2,108},{3,125},{4,98},{5,115},{6,96},{7,113},{8,1... | collective-permute-start | bytes 405512 | tf_op jit(solution)/shard_map/ppermute | solution.py:273
  18.0 10.2 %collective-permute-start.1 = (f32[264,128]{1,0:T(8,128)}, f32[264,128]{1,0:T(8,128)S(1)}, u32[]{:S(2)}, u32[]{:S(2)}) collective-permute-start(f32[264,128]{1,0:T(8,128)} %shard_map.55.refs_0_), channel_id=1, source_target_pairs={{0,38},{1,55},{2,36},{3,53},{4,42},{5,59},{6,40},{7,57},{8,46},{9,... | collective-permute-start | bytes 405512 | tf_op jit(solution)/shard_map/ppermute | solution.py:273
  19.6 12.3 %collective-permute-start = (f32[264,128]{1,0:T(8,128)}, f32[264,128]{1,0:T(8,128)S(1)}, u32[]{:S(2)}, u32[]{:S(2)}) collective-permute-start(f32[264,128]{1,0:T(8,128)} %shard_map.55.refs_0_), channel_id=1, source_target_pairs={{0,66},{1,83},{2,64},{3,81},{4,70},{5,87},{6,68},{7,85},{8,74},{9,... | collective-permute-start | bytes 405512 | tf_op jit(solution)/shard_map/ppermute | solution.py:273
  23.1 8.8 %collective-permute-start.14 = (f32[264,128]{1,0:T(8,128)S(1)}, f32[264,128]{1,0:T(8,128)S(1)}, u32[]{:S(2)}, u32[]{:S(2)}) collective-permute-start(f32[264,128]{1,0:T(8,128)S(1)} %collective-permute-done.6.refs_7_), channel_id=1, source_target_pairs={{0,1},{1,0},{2,3},{3,2},{4,5},{5,4},{6,7},{7,6},{8,9},{9,8},{10,11... | collective-permute-start | bytes 405512 | tf_op jit(solution)/shard_map/ppermute | solution.py:275
  23.1 9.3 %collective-permute-start.13 = (f32[264,128]{1,0:T(8,128)S(1)}, f32[264,128]{1,0:T(8,128)S(1)}, u32[]{:S(2)}, u32[]{:S(2)}) collective-permute-start(f32[264,128]{1,0:T(8,128)S(1)} %collective-permute-done.5.refs_6_), channel_id=1, source_target_pairs={{0,1},{1,0},{2,3},{3,2},{4,5},{5,4},{6,7},{7,6},{8,9},{9,8},{10,11... | collective-permute-start | bytes 405512 | tf_op jit(solution)/shard_map/ppermute | solution.py:275
  23.7 8.8 %collective-permute-start.12 = (f32[264,128]{1,0:T(8,128)S(1)}, f32[264,128]{1,0:T(8,128)S(1)}, u32[]{:S(2)}, u32[]{:S(2)}) collective-permute-start(f32[264,128]{1,0:T(8,128)S(1)} %collective-permute-done.4.refs_5_), channel_id=1, source_target_pairs={{0,1},{1,0},{2,3},{3,2},{4,5},{5,4},{6,7},{7,6},{8,9},{9,8},{10,11... | collective-permute-start | bytes 405512 | tf_op jit(solution)/shard_map/ppermute | solution.py:275
  28.2 4.7 %collective-permute-start.11 = (f32[264,128]{1,0:T(8,128)S(1)}, f32[264,128]{1,0:T(8,128)S(1)}, u32[]{:S(2)}, u32[]{:S(2)}) collective-permute-start(f32[264,128]{1,0:T(8,128)S(1)} %collective-permute-done.3.refs_4_), channel_id=1, source_target_pairs={{0,1},{1,0},{2,3},{3,2},{4,5},{5,4},{6,7},{7,6},{8,9},{9,8},{10,11... | collective-permute-start | bytes 405512 | tf_op jit(solution)/shard_map/ppermute | solution.py:275
  31.9 1.4 %collective-permute-start.10 = (f32[264,128]{1,0:T(8,128)S(1)}, f32[264,128]{1,0:T(8,128)S(1)}, u32[]{:S(2)}, u32[]{:S(2)}) collective-permute-start(f32[264,128]{1,0:T(8,128)S(1)} %collective-permute-done.2.refs_3_), channel_id=1, source_target_pairs={{0,1},{1,0},{2,3},{3,2},{4,5},{5,4},{6,7},{7,6},{8,9},{9,8},{10,11... | collective-permute-start | bytes 405512 | tf_op jit(solution)/shard_map/ppermute | solution.py:275
  31.9 1.5 %collective-permute-start.9 = (f32[264,128]{1,0:T(8,128)S(1)}, f32[264,128]{1,0:T(8,128)S(1)}, u32[]{:S(2)}, u32[]{:S(2)}) collective-permute-start(f32[264,128]{1,0:T(8,128)S(1)} %collective-permute-done.1.refs_2_), channel_id=1, source_target_pairs={{0,1},{1,0},{2,3},{3,2},{4,5},{5,4},{6,7},{7,6},{8,9},{9,8},{10,11... | collective-permute-start | bytes 405512 | tf_op jit(solution)/shard_map/ppermute | solution.py:275
  32.4 1.4 %collective-permute-start.8 = (f32[264,128]{1,0:T(8,128)S(1)}, f32[264,128]{1,0:T(8,128)S(1)}, u32[]{:S(2)}, u32[]{:S(2)}) collective-permute-start(f32[264,128]{1,0:T(8,128)S(1)} %collective-permute-done.refs_1_), channel_id=1, source_target_pairs={{0,1},{1,0},{2,3},{3,2},{4,5},{5,4},{6,7},{7,6},{8,9},{9,8},{10,11... | collective-permute-start | bytes 405512 | tf_op jit(solution)/shard_map/ppermute | solution.py:275
  33.8 0.9 %copy-start = (f32[264,128]{1,0:T(8,128)S(1)}, f32[264,128]{1,0:T(8,128)}, u32[]{:S(2)}) copy-start(f32[264,128]{1,0:T(8,128)} %shard_map.55.refs_0_) | copy-start | bytes 405508

commit v2 on v1

v2 whole, which is shorter than its diff:
```python
import jax
import jax.numpy as jnp
import numpy as np
from jax import lax
from jax.experimental import pallas as pl
from jax.experimental.pallas import tpu as pltpu
from jax.sharding import PartitionSpec as P

ORDER = 4
NODES = 64
ITERS = 2
FIELDS = 4
SLICES = 8
LAYERS = 16
CELLS = 128
ROWS = FIELDS * NODES
PART = ROWS + 8
PAIR = 2 * PART + 8
DEGREE = 22
BASE_STEP = 0.015

OFFSETS = (
    (((2, 1), (0, 0)), ((2, 0), (0, 0))),
    (((1, 0), (0, 0)), ((3, 0), (0, 0))),
    (((1, 1), (1, 1)), ((3, 1), (1, 0))),
    (((0, 1), (0, 1)), None),
)
EARLY = 2


def modal_tables():
    points = np.array([-1.0, -1.0 / np.sqrt(5.0), 1.0 / np.sqrt(5.0), 1.0])
    to_nodes = np.polynomial.legendre.legvander(points, ORDER - 1)
    to_modes = np.linalg.inv(to_nodes)
    cube = lambda m: np.kron(np.kron(m, m), m).astype(np.float32)
    return cube(to_modes), cube(to_nodes)


def route(move):
    pairs = []
    for x in range(4):
        for high in range(2):
            for y in range(4):
                for low in range(2):
                    for core in range(2):
                        target = move(x, high, y, low, core)
                        if target is None:
                            continue
                        to_x, to_high, to_y, to_low, to_core = target
                        source = (x * 2 + high) * 16 + y * 4 + low * 2 + core
                        place = (to_x % 4 * 2 + to_high % 2) * 16 + to_y % 4 * 4 + to_low % 2 * 2 + to_core % 2
                        pairs.append((source, place))
    return pairs


def prepare_kernel(step_ref, state_ref, other_ref, near_ref, near_other_ref, table_ref, out_ref, copy_ref):
    table = table_ref[...]
    core = lax.axis_index("space") % 2
    for k, (state, near) in enumerate(((state_ref, near_ref), (other_ref, near_other_ref))):
        base = pl.multiple_of((core if k == 0 else 1 - core) * PART, 8)
        for field in range(FIELDS):
            value = jnp.dot(
                table,
                state[pl.ds(field * NODES, NODES), :],
                precision=lax.Precision.HIGHEST,
                preferred_element_type=jnp.float32,
            )
            rows = pl.ds(base + field * NODES, NODES)
            out_ref[rows, :] = value
            copy_ref[rows, :] = value
        tail = jnp.concatenate([near[f].astype(jnp.float32) for f in (0, 1, 2, 3, 4, 5, 5, 5)], axis=0)
        rows = pl.ds(base + ROWS, 8)
        out_ref[rows, :] = tail
        copy_ref[rows, :] = tail
    lane = lax.broadcasted_iota(jnp.int32, (8, CELLS), 1)
    count = jnp.where(lane == lax.axis_index("tm"), step_ref[0], 0).astype(jnp.float32)
    out_ref[pl.ds(2 * PART, 8), :] = count
    copy_ref[pl.ds(2 * PART, 8), :] = count


def count_kernel(step_ref, far_ref, pair_any, out_any, counts, sem):
    lane = lax.broadcasted_iota(jnp.int32, (8, CELLS), 1)
    own = lax.axis_index("tm")
    far = (own // 2 + 2) % 4 * 2 + own % 2
    count = jnp.where(lane == own, step_ref[0], jnp.where(lane == far, far_ref[0], 0))
    counts[...] = count.astype(jnp.float32)
    copy = pltpu.make_async_copy(counts, out_any.at[pl.ds(2 * PART, 8), :], sem)
    copy.start()
    copy.wait()


def ends(p, u):
    m = (u[0] + u[2]) + (p[1] + p[3])
    n = (p[0] + p[2]) + (u[1] + u[3])
    return m - n, m + n


def rates(p, u, d_x, d_y):
    o_u = u[1] + u[3]
    o_p = p[1] + p[3]
    p_0 = 0.25 * (d_y - d_x)
    u_0 = 0.25 * (d_x + d_y)
    t = u_0 + o_p
    w = p_0 + o_u
    rate_p = [p_0, -3.0 * (t + u[2]), 5.0 * (p_0 + u[1]), -3.0 * t]
    rate_u = [u_0, -3.0 * (w + p[2]), 5.0 * (u_0 + p[1]), -3.0 * w]
    return rate_p, rate_u


def lanes(value, index):
    return jnp.take_along_axis(value, index, axis=1, mode="promise_in_bounds")


def row(field, a, b, c, v):
    return (field * NODES + a * 16 + b * 4 + c) * LAYERS + v * 8


def apply_operator(src, dst, index_ref):
    get = lambda r: src[pl.ds(r, 8), :]

    def put(r, value):
        dst[pl.ds(r, 8), :] = value

    index = lambda face, v: index_ref[pl.ds(face * LAYERS + v * 8, 8), :]
    four = range(ORDER)
    for b in four:
        low = [[ends([get(row(0, a, b, c, v)) for a in four], [get(row(1, a, b, c, v)) for a in four]) for c in four] for v in range(2)]
        near_x = [
            [lanes(low[1][c][0], index(1, 0)) for c in four],
            [lanes(pltpu.roll(low[0][c][0], 7, 0), index(1, 1)) for c in four],
        ]
        near_y = [
            [lanes(pltpu.roll(low[1][c][1], 1, 0), index(0, 0)) for c in four],
            [lanes(low[0][c][1], index(0, 1)) for c in four],
        ]
        for v in range(2):
            for c in four:
                p = [get(row(0, a, b, c, v)) for a in four]
                u = [get(row(1, a, b, c, v)) for a in four]
                rate_p, rate_u = rates(p, u, near_x[v][c] - low[v][c][0], near_y[v][c] - low[v][c][1])
                for a in four:
                    put(row(0, a, b, c, v), rate_p[a])
                    put(row(1, a, b, c, v), rate_u[a])
    for v in range(2):
        for a in four:
            rate = [[None] * ORDER for _ in four]
            column = lambda c: ([get(row(0, a, b, c, v)) for b in four], [get(row(2, a, b, c, v)) for b in four])
            line = lambda b: ([get(row(0, a, b, c, v)) for c in four], [get(row(3, a, b, c, v)) for c in four])
            low_y = [ends(*column(c)) for c in four]
            low_z = [ends(*line(b)) for b in four]
            x_y = [lanes(low_y[c][0], index(3, v)) - low_y[c][0] for c in four]
            y_y = [lanes(low_y[c][1], index(2, v)) - low_y[c][1] for c in four]
            x_z = [lanes(low_z[b][0], index(5, v)) - low_z[b][0] for b in four]
            y_z = [lanes(low_z[b][1], index(4, v)) - low_z[b][1] for b in four]
            for c in four:
                rate_p, rate_u = rates(*column(c), x_y[c], y_y[c])
                for b in four:
                    rate[b][c] = rate_p[b]
                    put(row(2, a, b, c, v), rate_u[b])
            for b in four:
                rate_p, rate_u = rates(*line(b), x_z[b], y_z[b])
                for c in four:
                    r = row(0, a, b, c, v)
                    put(r, dst[pl.ds(r, 8), :] + (rate[b][c] + rate_p[c]))
                    put(row(3, a, b, c, v), rate_u[c])


def coefficients(counts):
    lane = lax.broadcasted_iota(jnp.int32, (8, CELLS), 1)
    wide = jnp.broadcast_to(counts, (8, CELLS))
    steps = [jnp.broadcast_to(wide[:, n : n + 1], (8, CELLS)) * BASE_STEP for n in range(SLICES)]
    image = lambda value: pltpu.roll(value, 1, 1)
    twice = lambda value: pltpu.roll(value, 2, 1)
    initial = jnp.where(lane == 0, 1.0, 0.0)
    states = [(initial, initial, initial)] * SLICES
    for _ in range(ITERS):
        begin = initial
        fresh = []
        for n in range(SLICES):
            h = steps[n]
            u_0, u_1, u_2 = states[n]
            old_0, old_1, old_2 = image(u_0), image(u_1), image(u_2)
            first = u_0 + h * (5.0 / 24.0 * old_0 + 1.0 / 3.0 * old_1 - 1.0 / 24.0 * old_2)
            image_first = image(first)
            second = (
                first
                + h * (image_first - old_1)
                + h * (-1.0 / 24.0 * old_0 + 1.0 / 3.0 * old_1 + 5.0 / 24.0 * old_2)
            )
            image_second = image(second)
            correction = h * (2.0 / 3.0 * image_first - 1.0 / 3.0 * old_0 - 1.0 / 3.0 * image_second)
            carried = h * (0.5 * image_second - 0.5 * old_0) + correction
            offset = 0.5 * h * image(carried) + correction
            finish = begin + h * image(begin) + 0.5 * h * h * twice(begin) + offset
            fresh.append((begin, first + 0.5 * ((begin - u_0) + (finish - second)), finish))
            begin = finish
        states = fresh
    return states


def advance_kernel(*refs):
    pairs = refs[:9]
    table_ref, out_ref, one, two, index_ref, saved, coef_ref, spread_ref, sum_ref = refs[9:]
    space = lax.axis_index("space")
    core = space % 2
    chip = space // 2
    low = chip % 2
    high = chip // 2
    counts = jnp.zeros((1, CELLS), jnp.float32)

    def take(pair, step_y, step_z):
        place = (high + 4 - step_y) % 4 * 2 + (low + step_z) % 2
        for half in range(2):
            base = place + 8 * half
            for m in range(ROWS // 8):
                one[pl.ds(m * 8 * LAYERS + base, 8, stride=LAYERS), :] = pair[pl.ds(half * PART + m * 8, 8), :]
            tail = pair[pl.ds(half * PART + ROWS, 8), :]
            for face in range(6):
                index_ref[pl.ds(face * LAYERS + base, 1), :] = tail[face : face + 1].astype(jnp.int32)

    take(pairs[0], 0, 0)
    for k, (zero, first) in enumerate(OFFSETS):
        if first is None:

            @pl.when(core == 0)
            def _():
                take(pairs[1 + k], *zero[0])

            @pl.when(core == 1)
            def _():
                take(pairs[5 + k], *zero[0])
        else:
            for swapped in range(2):
                on_zero = core == swapped
                step_y = jnp.where(on_zero, zero[0][0], first[0][0])
                step_z = jnp.where(on_zero, zero[0][1], first[0][1])
                take(pairs[1 + 4 * swapped + k], step_y, step_z)
    for pair in pairs:
        counts = jnp.maximum(counts, pair[pl.ds(2 * PART, 1), :])

    polynomials = coefficients(counts)
    for n in range(SLICES):
        for m in range(3):
            coef_ref[pl.ds((n * 3 + m) * 8, 8), :] = polynomials[n][m]
    own_slice = lax.axis_index("tm")
    for m in range(3):
        mine = coef_ref[pl.ds(pl.multiple_of((own_slice * 3 + m) * 8, 8), 8), :]
        for k in range(DEGREE + 1):
            spread_ref[pl.ds((k * 3 + m) * 8, 8), :] = jnp.broadcast_to(mine[:, k : k + 1], (8, CELLS))

    own = core * 8 + chip

    def keep(source, k):
        for m in range(ROWS // 8):
            saved[pl.ds(k * ROWS + m * 8, 8), :] = source[pl.ds(m * 8 * LAYERS + own, 8, stride=LAYERS), :]

    keep(one, 0)

    def advance(turn, carry):
        apply_operator(one, two, index_ref)
        keep(two, 2 * turn + 1)
        apply_operator(two, one, index_ref)
        keep(one, 2 * turn + 2)
        return carry

    lax.fori_loop(0, DEGREE // 2, advance, 0)

    group = 16

    def combine(g, carry):
        total = [[None] * group for _ in range(3)]
        for k in range(DEGREE + 1):
            value = [saved[pl.ds(k * ROWS + (g * group + i) * 8, 8), :] for i in range(group)]
            for m in range(3):
                factor = spread_ref[pl.ds((k * 3 + m) * 8, 8), :]
                for i in range(group):
                    term = factor * value[i]
                    total[m][i] = term if total[m][i] is None else total[m][i] + term
        for m in range(3):
            for i in range(group):
                sum_ref[pl.ds(m * ROWS + (g * group + i) * 8, 8), :] = total[m][i]
        return carry

    lax.fori_loop(0, ROWS // 8 // group, combine, 0)
    table = table_ref[...]
    for m in range(3 * FIELDS):
        rows = pl.ds(m * NODES, NODES)
        out_ref[rows, :] = jnp.dot(
            table, sum_ref[rows, :], precision=lax.Precision.HIGHEST, preferred_element_type=jnp.float32
        )


def shards(initial, neighbours, step_counts):
    to_modes, to_nodes = modal_tables()
    axes = ("tm", "space")
    swap = route(lambda x, high, y, low, core: (x, high, y, low, core + 1))
    one_way = route(lambda x, high, y, low, core: (x, high, y, low, 1) if core == 0 else None)
    far = lax.ppermute(step_counts, axes, route(lambda x, high, y, low, core: (x + 2, high, y, low, core)))
    state = initial.reshape(ROWS, CELLS)
    other = lax.ppermute(state, axes, swap)
    near_other = lax.ppermute(neighbours, axes, swap)
    whole = lambda: pl.BlockSpec(memory_space=pltpu.VMEM)
    anywhere = lambda: pl.BlockSpec(memory_space=pl.ANY)
    scalar = lambda: pl.BlockSpec(memory_space=pltpu.SMEM)
    pair, late = pl.pallas_call(
        prepare_kernel,
        out_shape=[jax.ShapeDtypeStruct((PAIR, CELLS), jnp.float32)] * 2,
        in_specs=[scalar()] + [whole() for _ in range(5)],
        out_specs=[whole(), whole()],
    )(step_counts, state, other, neighbours, near_other, jnp.asarray(to_modes))
    late = pl.pallas_call(
        count_kernel,
        out_shape=jax.ShapeDtypeStruct((PAIR, CELLS), jnp.float32),
        in_specs=[scalar(), scalar(), anywhere()],
        out_specs=anywhere(),
        scratch_shapes=[pltpu.VMEM((8, CELLS), jnp.float32), pltpu.SemaphoreType.DMA],
        input_output_aliases={2: 0},
    )(step_counts, far, late)

    direct = []
    for k, entry in enumerate(OFFSETS):

        def move(x, high, y, low, core):
            if entry[core] is None:
                return None
            (step_y, step_z), (skew_x, skew_z) = entry[core]
            return (x + skew_x, high + skew_z, y + step_y, low + step_z, core)

        direct.append(lax.ppermute(pair if k < EARLY else late, axes, route(move)))
    own = lax.ppermute(late, axes, swap)
    swapped = [
        lax.ppermute(value, axes, one_way if entry[1] is None else swap) for value, entry in zip(direct, OFFSETS)
    ]
    pairs = [own] + direct + swapped

    result = pl.pallas_call(
        advance_kernel,
        out_shape=jax.ShapeDtypeStruct((3 * ROWS, CELLS), jnp.float32),
        in_specs=[whole() for _ in range(10)],
        out_specs=whole(),
        scratch_shapes=[
            pltpu.VMEM((ROWS * LAYERS, CELLS), jnp.float32),
            pltpu.VMEM((ROWS * LAYERS, CELLS), jnp.float32),
            pltpu.VMEM((6 * LAYERS, CELLS), jnp.int32),
            pltpu.VMEM(((DEGREE + 1) * ROWS, CELLS), jnp.float32),
            pltpu.VMEM((SLICES * 3 * 8, CELLS), jnp.float32),
            pltpu.VMEM(((DEGREE + 1) * 3 * 8, CELLS), jnp.float32),
            pltpu.VMEM((3 * ROWS, CELLS), jnp.float32),
        ],
        compiler_params=pltpu.CompilerParams(vmem_limit_bytes=32 * 1024 * 1024),
    )(*pairs, jnp.asarray(to_nodes))
    return result.reshape(1, 3, FIELDS, NODES, 1, CELLS)


def solution(mesh):
    placed = (P(None, None, "space", None), P(None, "space", None), P("tm"))
    return jax.shard_map(
        shards,
        mesh=mesh,
        in_specs=placed,
        out_specs=P("tm", None, None, None, "space", None),
        check_vma=False,
    )
```

time: 55.9 us -> 49.6 us (0.89)
  waiting for transfers between devices: 6.82 us -> 1.19 us
  starting transfers between devices: 23.2 us -> 25.5 us
  Pallas kernels: 22.9 us -> 20.8 us
  local copies, waits for them, and re-layouts: 2.19 us -> 1.22 us
    ppermute x15 -> x12, waiting for transfers between devices: 6.82 us -> 1.19 us  [the longest x4 1.16 us: shards(): lax.ppermute(value, axes, one_way if entry[1] is None else swap)]
    pallas_call x1, Pallas kernels: 21.1 us -> 17.4 us  [shards(): pl.pallas_call(advance_kernel, out_shape=jax.ShapeDtypeStruct((3 * ROWS,...]
    ppermute x15 -> x12, starting transfers between devices: 23.2 us -> 25.5 us  [the longest x4 10.7 us: shards(): lax.ppermute(value, axes, one_way if entry[1] is None else swap)]
    pallas_call x1 -> x2, Pallas kernels: 1.82 us -> 3.35 us  [the longest x1 2.11 us: shards(): pl.pallas_call(prepare_kernel, out_shape=[jax.ShapeDtypeStruct((PAIR, CEL...]
    unnamed x5 -> x8, local copies, waits for them, and re-layouts: 2.19 us -> 1.22 us
  transfers between devices with their start and end apart: 15 -> 12, of which waited for: 6 -> 1; matrix products, arithmetic and copies ran while one was open for 0% -> 0% of each run, Pallas kernels for 0% -> 4%
where the time goes in v2:
time: 49.6 us; the launch traced here: 49.4 us
  starting transfers between devices  25.5 us (51%)
  Pallas kernels  20.8 us (42%)
  local copies, waits for them, and re-layouts  1.22 us (2%)
  waiting for transfers between devices  1.19 us (2%)
  between operations  0.77 us (2%)
    pallas_call x1, Pallas kernels, shards(): pl.pallas_call(advance_kernel, out_shape=jax.ShapeDtypeStruct((3 * ROWS,...  17.4 us
    ppermute x4, starting transfers between devices, shards(): lax.ppermute(value, axes, one_way if entry[1] is None else swap)  10.7 us
    ppermute x4, starting transfers between devices, shards(): direct.append(lax.ppermute(pair if k < EARLY else late, axes, route(move)))  5.38 us
    ppermute x1, starting transfers between devices, shards(): own = lax.ppermute(late, axes, swap)  5.22 us
    ppermute x1, starting transfers between devices, shards(): lax.ppermute(step_counts, axes, route(lambda x, high, y, low, core: (x +...  2.83 us
    pallas_call x1, Pallas kernels, shards(): pl.pallas_call(prepare_kernel, out_shape=[jax.ShapeDtypeStruct((PAIR, CEL...  2.11 us
    ppermute x1, starting transfers between devices, shards(): other = lax.ppermute(state, axes, swap)  1.42 us
    pallas_call x1, Pallas kernels, shards(): pl.pallas_call(count_kernel, out_shape=jax.ShapeDtypeStruct((PAIR, CELLS)...  1.24 us
  transfers between devices with their start and end apart: 12, of which 1 were waited for; matrix products, arithmetic and copies ran while one was open for 0% of the time, Pallas kernels for 4%

profile of v2, /device:TPU:1, one launch (start us, length us, event | category | flops | bytes accessed | tf_op | source)
XLA Modules:
  0.0 49.4 jit_solution(6366426762483598224)
XLA Ops:
  0.0 1.4 %collective-permute-start.1 = (f32[256,128]{1,0:T(8,128)}, f32[256,128]{1,0:T(8,128)S(1)}, u32[]{:S(2)}, u32[]{:S(2)}) collective-permute-start(f32[256,128]{1,0:T(8,128)} %bitcast.4), channel_id=1, source_target_pairs={{0,1},{1,0},{2,3},{3,2},{4,5},{5,4},{6,7},{7,6},{8,9},{9,8},{10,11... | collective-permute-start | bytes 393224 | tf_op jit(solution)/shard_map/ppermute | solution.py:300
  1.4 0.0 collective-permute-start.2
  1.4 2.8 %collective-permute-start = (s32[1]{0:T(128)}, s32[1]{0:T(128)}, u32[]{:S(2)}, u32[]{:S(2)}) collective-permute-start(s32[1]{0:T(128)} %param.7), channel_id=1, source_target_pairs={{0,64},{1,65},{2,66},{3,67},{4,68},{5,69},{6,70},{7,71},{8,72},{9,... | collective-permute-start | bytes 20 | tf_op jit(solution)/shard_map/ppermute | solution.py:298
  4.9 0.0 collective-permute-done.2.near_other_ref
  4.9 0.0 copy-start.2
  5.0 0.0 collective-permute-done.1.other_ref
  5.0 0.6 %copy-done.2 = s32[6,1,128]{2,1,0:T(1,128)} copy-done((s32[6,1,128]{2,1,0:T(1,128)}, s32[6,1,128]{2,1,0:T(1,128)S(1)}, u32[]{:S(2)}) %copy-start.2) | copy-done | bytes 3096
  5.5 0.6 %copy-done.1 = f32[256,128]{1,0:T(8,128)} copy-done((f32[256,128]{1,0:T(8,128)}, f32[256,128]{1,0:T(8,128)S(1)}, u32[]{:S(2)}) %copy-start.1) | copy-done | bytes 131096
  6.2 2.1 %shard_map.55 = (f32[536,128]{1,0:T(8,128)}, f32[536,128]{1,0:T(8,128)}) custom-call(s32[1]{0:T(128)S(6)} %copy.9.step_ref, f32[256,128]{1,0:T(8,128)} %bitcast.5, f32[256,128]{1,0:T(8,128)} %copy-done.1, s32[6,1,128]{2,1,0:T(1,128)} %near_ref.1, s32[6,1,128]{2,1,0:T(1,128)} %copy-done.2, f32[64,64]{1,0:T(8,128)} %constant.4.clone.table_ref), custom_call_target="tpu_custom_call" | custom-call | tf_op jit(solution)/shard_map/pallas_call | solution.py:305
  8.3 0.0 collective-permute-done.far_ref
  8.3 1.2 %shard_map.56 = f32[536,128]{1,0:T(8,128)} custom-call(s32[1]{0:T(128)S(6)} %copy.9.step_ref, s32[1]{0:T(128)} %collective-permute-done.far_ref, f32[536,128]{1,0:T(8,128)} %get-tuple-element.7.pair_any), custom_call_target="tpu_custom_call", output_to_operand_aliasing={{}: (2, {})} | custom-call | tf_op jit(solution)/shard_map/pallas_call | solution.py:311
  9.6 0.7 %collective-permute-start.7 = (f32[536,128]{1,0:T(8,128)}, f32[536,128]{1,0:T(8,128)S(1)}, u32[]{:S(2)}, u32[]{:S(2)}) collective-permute-start(f32[536,128]{1,0:T(8,128)} %shard_map.56), channel_id=1, source_target_pairs={{0,18},{2,16},{4,22},{6,20},{8,26},{10,24},{12,30},{14,28},{16,2},... | collective-permute-start | bytes 823304 | tf_op jit(solution)/shard_map/ppermute | solution.py:329
  10.2 4.2 %collective-permute-start.6 = (f32[536,128]{1,0:T(8,128)}, f32[536,128]{1,0:T(8,128)S(1)}, u32[]{:S(2)}, u32[]{:S(2)}) collective-permute-start(f32[536,128]{1,0:T(8,128)} %shard_map.56), channel_id=1, source_target_pairs={{0,54},{1,47},{2,52},{3,45},{4,58},{5,35},{6,56},{7,33},{8,62},{9,... | collective-permute-start | bytes 823304 | tf_op jit(solution)/shard_map/ppermute | solution.py:329
  14.4 0.0 copy-done.3
  14.4 0.5 collective-permute-start.5
  14.9 0.1 collective-permute-start.4
  14.9 5.2 %collective-permute-start.3 = (f32[536,128]{1,0:T(8,128)}, f32[536,128]{1,0:T(8,128)S(1)}, u32[]{:S(2)}, u32[]{:S(2)}) collective-permute-start(f32[536,128]{1,0:T(8,128)} %shard_map.56), channel_id=1, source_target_pairs={{0,1},{1,0},{2,3},{3,2},{4,5},{5,4},{6,7},{7,6},{8,9},{9,8},{10,11... | collective-permute-start | bytes 823304 | tf_op jit(solution)/shard_map/ppermute | solution.py:330
  20.2 0.0 collective-permute-done.7.refs_4_
  20.2 1.3 %collective-permute-start.11 = (f32[536,128]{1,0:T(8,128)S(1)}, f32[536,128]{1,0:T(8,128)S(1)}, u32[]{:S(2)}, u32[]{:S(2)}) collective-permute-start(f32[536,128]{1,0:T(8,128)S(1)} %collective-permute-done.7.refs_4_), channel_id=1, source_target_pairs={{0,1},{2,3},{4,5},{6,7},{8,9},{10,11},{12,13},{14,15},{16,17},{18,... | collective-permute-start | bytes 823304 | tf_op jit(solution)/shard_map/ppermute | solution.py:332
  21.5 0.0 collective-permute-done.6.refs_3_
  21.5 7.1 %collective-permute-start.10 = (f32[536,128]{1,0:T(8,128)S(1)}, f32[536,128]{1,0:T(8,128)S(1)}, u32[]{:S(2)}, u32[]{:S(2)}) collective-permute-start(f32[536,128]{1,0:T(8,128)S(1)} %collective-permute-done.6.refs_3_), channel_id=1, source_target_pairs={{0,1},{1,0},{2,3},{3,2},{4,5},{5,4},{6,7},{7,6},{8,9},{9,8},{10,11... | collective-permute-start | bytes 823304 | tf_op jit(solution)/shard_map/ppermute | solution.py:332
  28.6 0.0 collective-permute-done.5.refs_2_
  28.6 0.0 collective-permute-start.9
  28.6 0.0 collective-permute-done.4.refs_1_
  28.6 2.2 %collective-permute-start.8 = (f32[536,128]{1,0:T(8,128)S(1)}, f32[536,128]{1,0:T(8,128)S(1)}, u32[]{:S(2)}, u32[]{:S(2)}) collective-permute-start(f32[536,128]{1,0:T(8,128)S(1)} %collective-permute-done.4.refs_1_), channel_id=1, source_target_pairs={{0,1},{1,0},{2,3},{3,2},{4,5},{5,4},{6,7},{7,6},{8,9},{9,8},{10,11... | collective-permute-start | bytes 823304 | tf_op jit(solution)/shard_map/ppermute | solution.py:332
  30.9 0.0 collective-permute-done.3.refs_0_
  30.9 0.0 collective-permute-done.11.refs_8_
  30.9 0.0 collective-permute-done.10.refs_7_
  30.9 0.0 collective-permute-done.9.refs_6_
  30.9 1.2 %collective-permute-done.8.refs_5_ = f32[536,128]{1,0:T(8,128)S(1)} collective-permute-done((f32[536,128]{1,0:T(8,128)S(1)}, f32[536,128]{1,0:T(8,128)S(1)}, u32[]{:S(2)}, u32[]{:S(2)}) %collective-permute-start.8) | collective-permute-done | bytes 274464 | tf_op jit(solution)/shard_map/ppermute | solution.py:332
  32.0 0.0 copy-done
  32.0 17.4 %shard_map.57 = f32[768,128]{1,0:T(8,128)} custom-call(f32[536,128]{1,0:T(8,128)S(1)} %collective-permute-done.3.refs_0_, f32[536,128]{1,0:T(8,128)S(1)} %collective-permute-done.4.refs_1_, f32[536,128]{1,0:T(8,128)S(1)} %collective-permute-done.5.refs_2_, f32[536,128]{1,0:T(8,128)S(1)} %collective-permute-done.6.refs_3_, ...), custom_call_target="tpu_custom_call" | custom-call | tf_op jit(solution)/shard_map/pallas_call | solution.py:336
  (3 shorter events, 0.0 us)
Async XLA Ops:
  0.0 5.0 %collective-permute-start.1 = (f32[256,128]{1,0:T(8,128)}, f32[256,128]{1,0:T(8,128)S(1)}, u32[]{:S(2)}, u32[]{:S(2)}) collective-permute-start(f32[256,128]{1,0:T(8,128)} %bitcast.4), channel_id=1, source_target_pairs={{0,1},{1,0},{2,3},{3,2},{4,5},{5,4},{6,7},{7,6},{8,9},{9,8},{10,11... | collective-permute-start | bytes 393224 | tf_op jit(solution)/shard_map/ppermute | solution.py:300
  1.4 3.5 %collective-permute-start.2 = (s32[6,1,128]{2,1,0:T(1,128)}, s32[6,1,128]{2,1,0:T(1,128)S(1)}, u32[]{:S(2)}, u32[]{:S(2)}) collective-permute-start(s32[6,1,128]{2,1,0:T(1,128)} %near_ref.1), channel_id=1, source_target_pairs={{0,1},{1,0},{2,3},{3,2},{4,5},{5,4},{6,7},{7,6},{8,9},{9,8},{10,11... | collective-permute-start | bytes 9224 | tf_op jit(solution)/shard_map/ppermute | solution.py:301
  1.4 6.9 %collective-permute-start = (s32[1]{0:T(128)}, s32[1]{0:T(128)}, u32[]{:S(2)}, u32[]{:S(2)}) collective-permute-start(s32[1]{0:T(128)} %param.7), channel_id=1, source_target_pairs={{0,64},{1,65},{2,66},{3,67},{4,68},{5,69},{6,70},{7,71},{8,72},{9,... | collective-permute-start | bytes 20 | tf_op jit(solution)/shard_map/ppermute | solution.py:298
  4.9 0.6 %copy-start.2 = (s32[6,1,128]{2,1,0:T(1,128)}, s32[6,1,128]{2,1,0:T(1,128)S(1)}, u32[]{:S(2)}) copy-start(s32[6,1,128]{2,1,0:T(1,128)S(1)} %collective-permute-done.2.near_other_ref) | copy-start | bytes 9220
  5.5 0.7 %copy-start.1 = (f32[256,128]{1,0:T(8,128)}, f32[256,128]{1,0:T(8,128)S(1)}, u32[]{:S(2)}) copy-start(f32[256,128]{1,0:T(8,128)S(1)} %collective-permute-done.1.other_ref) | copy-start | bytes 393220
  8.3 6.1 %copy-start.3 = (f32[536,128]{1,0:T(8,128)S(1)}, f32[536,128]{1,0:T(8,128)}, u32[]{:S(2)}) copy-start(f32[536,128]{1,0:T(8,128)} %get-tuple-element.8) | copy-start | bytes 823300
  8.3 23.7 %copy-start = (f32[64,64]{1,0:T(8,128)S(1)}, f32[64,64]{1,0:T(8,128)}, u32[]{:S(2)}) copy-start(f32[64,64]{1,0:T(8,128)} %constant.5.clone.refs_9_) | copy-start | bytes 49156
  9.6 10.6 %collective-permute-start.7 = (f32[536,128]{1,0:T(8,128)}, f32[536,128]{1,0:T(8,128)S(1)}, u32[]{:S(2)}, u32[]{:S(2)}) collective-permute-start(f32[536,128]{1,0:T(8,128)} %shard_map.56), channel_id=1, source_target_pairs={{0,18},{2,16},{4,22},{6,20},{8,26},{10,24},{12,30},{14,28},{16,2},... | collective-permute-start | bytes 823304 | tf_op jit(solution)/shard_map/ppermute | solution.py:329
  10.2 11.2 %collective-permute-start.6 = (f32[536,128]{1,0:T(8,128)}, f32[536,128]{1,0:T(8,128)S(1)}, u32[]{:S(2)}, u32[]{:S(2)}) collective-permute-start(f32[536,128]{1,0:T(8,128)} %shard_map.56), channel_id=1, source_target_pairs={{0,54},{1,47},{2,52},{3,45},{4,58},{5,35},{6,56},{7,33},{8,62},{9,... | collective-permute-start | bytes 823304 | tf_op jit(solution)/shard_map/ppermute | solution.py:329
  14.4 14.2 %collective-permute-start.5 = (f32[536,128]{1,0:T(8,128)S(1)}, f32[536,128]{1,0:T(8,128)S(1)}, u32[]{:S(2)}, u32[]{:S(2)}) collective-permute-start(f32[536,128]{1,0:T(8,128)S(1)} %copy-done.3), channel_id=1, source_target_pairs={{0,4},{1,13},{2,6},{3,15},{4,8},{5,1},{6,10},{7,3},{8,12},{9,5},{1... | collective-permute-start | bytes 823304 | tf_op jit(solution)/shard_map/ppermute | solution.py:329
  14.9 13.7 %collective-permute-start.4 = (f32[536,128]{1,0:T(8,128)S(1)}, f32[536,128]{1,0:T(8,128)S(1)}, u32[]{:S(2)}, u32[]{:S(2)}) collective-permute-start(f32[536,128]{1,0:T(8,128)S(1)} %copy-done.3), channel_id=1, source_target_pairs={{0,10},{1,9},{2,8},{3,11},{4,14},{5,13},{6,12},{7,15},{8,2},{9,1},... | collective-permute-start | bytes 823304 | tf_op jit(solution)/shard_map/ppermute | solution.py:329
  14.9 15.9 %collective-permute-start.3 = (f32[536,128]{1,0:T(8,128)}, f32[536,128]{1,0:T(8,128)S(1)}, u32[]{:S(2)}, u32[]{:S(2)}) collective-permute-start(f32[536,128]{1,0:T(8,128)} %shard_map.56), channel_id=1, source_target_pairs={{0,1},{1,0},{2,3},{3,2},{4,5},{5,4},{6,7},{7,6},{8,9},{9,8},{10,11... | collective-permute-start | bytes 823304 | tf_op jit(solution)/shard_map/ppermute | solution.py:330
  20.2 10.7 %collective-permute-start.11 = (f32[536,128]{1,0:T(8,128)S(1)}, f32[536,128]{1,0:T(8,128)S(1)}, u32[]{:S(2)}, u32[]{:S(2)}) collective-permute-start(f32[536,128]{1,0:T(8,128)S(1)} %collective-permute-done.7.refs_4_), channel_id=1, source_target_pairs={{0,1},{2,3},{4,5},{6,7},{8,9},{10,11},{12,13},{14,15},{16,17},{18,... | collective-permute-start | bytes 823304 | tf_op jit(solution)/shard_map/ppermute | solution.py:332
  21.5 9.4 %collective-permute-start.10 = (f32[536,128]{1,0:T(8,128)S(1)}, f32[536,128]{1,0:T(8,128)S(1)}, u32[]{:S(2)}, u32[]{:S(2)}) collective-permute-start(f32[536,128]{1,0:T(8,128)S(1)} %collective-permute-done.6.refs_3_), channel_id=1, source_target_pairs={{0,1},{1,0},{2,3},{3,2},{4,5},{5,4},{6,7},{7,6},{8,9},{9,8},{10,11... | collective-permute-start | bytes 823304 | tf_op jit(solution)/shard_map/ppermute | solution.py:332
  28.6 2.3 %collective-permute-start.9 = (f32[536,128]{1,0:T(8,128)S(1)}, f32[536,128]{1,0:T(8,128)S(1)}, u32[]{:S(2)}, u32[]{:S(2)}) collective-permute-start(f32[536,128]{1,0:T(8,128)S(1)} %collective-permute-done.5.refs_2_), channel_id=1, source_target_pairs={{0,1},{1,0},{2,3},{3,2},{4,5},{5,4},{6,7},{7,6},{8,9},{9,8},{10,11... | collective-permute-start | bytes 823304 | tf_op jit(solution)/shard_map/ppermute | solution.py:332
  28.6 3.4 %collective-permute-start.8 = (f32[536,128]{1,0:T(8,128)S(1)}, f32[536,128]{1,0:T(8,128)S(1)}, u32[]{:S(2)}, u32[]{:S(2)}) collective-permute-start(f32[536,128]{1,0:T(8,128)S(1)} %collective-permute-done.4.refs_1_), channel_id=1, source_target_pairs={{0,1},{1,0},{2,3},{3,2},{4,5},{5,4},{6,7},{7,6},{8,9},{9,8},{10,11... | collective-permute-start | bytes 823304 | tf_op jit(solution)/shard_map/ppermute | solution.py:332

commit v3 on v2

--- a/solution.py
+++ b/solution.py
@@ -1,3 +1,5 @@
+import functools
+
 import jax
 import jax.numpy as jnp
 import numpy as np
@@ -90,20 +92,22 @@
 
 
 def ends(p, u):
-    m = (u[0] + u[2]) + (p[1] + p[3])
-    n = (p[0] + p[2]) + (u[1] + u[3])
-    return m - n, m + n
-
-
-def rates(p, u, d_x, d_y):
-    o_u = u[1] + u[3]
-    o_p = p[1] + p[3]
+    o_p, o_u = p[1] + p[3], u[1] + u[3]
+    m = (u[0] + u[2]) + o_p
+    n = (p[0] + p[2]) + o_u
+    return m - n, m + n, o_p, o_u
+
+
+def rates(p, u, near_x, near_y, end):
+    x, y, o_p, o_u = end
+    d_x = near_x - x
+    d_y = near_y - y
     p_0 = 0.25 * (d_y - d_x)
     u_0 = 0.25 * (d_x + d_y)
     t = u_0 + o_p
     w = p_0 + o_u
-    rate_p = [p_0, -3.0 * (t + u[2]), 5.0 * (p_0 + u[1]), -3.0 * t]
-    rate_u = [u_0, -3.0 * (w + p[2]), 5.0 * (u_0 + p[1]), -3.0 * w]
+    rate_p = [p_0, -3.0 * (t + u[1]), 5.0 * (p_0 + u[0]), -3.0 * t]
+    rate_u = [u_0, -3.0 * (w + p[1]), 5.0 * (u_0 + p[0]), -3.0 * w]
     return rate_p, rate_u
 
 
@@ -123,42 +127,47 @@
 
     index = lambda face, v: index_ref[pl.ds(face * LAYERS + v * 8, 8), :]
     four = range(ORDER)
+    middle = (1, 2)
     for b in four:
-        low = [[ends([get(row(0, a, b, c, v)) for a in four], [get(row(1, a, b, c, v)) for a in four]) for c in four] for v in range(2)]
+        end = [
+            [ends([get(row(0, a, b, c, v)) for a in four], [get(row(1, a, b, c, v)) for a in four]) for c in four]
+            for v in range(2)
+        ]
         near_x = [
-            [lanes(low[1][c][0], index(1, 0)) for c in four],
-            [lanes(pltpu.roll(low[0][c][0], 7, 0), index(1, 1)) for c in four],
+            [lanes(end[1][c][0], index(1, 0)) for c in four],
+            [lanes(pltpu.roll(end[0][c][0], 7, 0), index(1, 1)) for c in four],
         ]
         near_y = [
-            [lanes(pltpu.roll(low[1][c][1], 1, 0), index(0, 0)) for c in four],
-            [lanes(low[0][c][1], index(0, 1)) for c in four],
+            [lanes(pltpu.roll(end[1][c][1], 1, 0), index(0, 0)) for c in four],
+            [lanes(end[0][c][1], index(0, 1)) for c in four],
         ]
         for v in range(2):
             for c in four:
-                p = [get(row(0, a, b, c, v)) for a in four]
-                u = [get(row(1, a, b, c, v)) for a in four]
-                rate_p, rate_u = rates(p, u, near_x[v][c] - low[v][c][0], near_y[v][c] - low[v][c][1])
+                p = [get(row(0, a, b, c, v)) for a in middle]
+                u = [get(row(1, a, b, c, v)) for a in middle]
+                rate_p, rate_u = rates(p, u, near_x[v][c], near_y[v][c], end[v][c])
                 for a in four:
                     put(row(0, a, b, c, v), rate_p[a])
                     put(row(1, a, b, c, v), rate_u[a])
     for v in range(2):
         for a in four:
+            p = [[get(row(0, a, b, c, v)) for c in four] for b in four]
             rate = [[None] * ORDER for _ in four]
-            column = lambda c: ([get(row(0, a, b, c, v)) for b in four], [get(row(2, a, b, c, v)) for b in four])
-            line = lambda b: ([get(row(0, a, b, c, v)) for c in four], [get(row(3, a, b, c, v)) for c in four])
-            low_y = [ends(*column(c)) for c in four]
-            low_z = [ends(*line(b)) for b in four]
-            x_y = [lanes(low_y[c][0], index(3, v)) - low_y[c][0] for c in four]
-            y_y = [lanes(low_y[c][1], index(2, v)) - low_y[c][1] for c in four]
-            x_z = [lanes(low_z[b][0], index(5, v)) - low_z[b][0] for b in four]
-            y_z = [lanes(low_z[b][1], index(4, v)) - low_z[b][1] for b in four]
+            end = [ends([p[b][c] for b in four], [get(row(2, a, b, c, v)) for b in four]) for c in four]
+            near_x = [lanes(end[c][0], index(3, v)) for c in four]
+            near_y = [lanes(end[c][1], index(2, v)) for c in four]
             for c in four:
-                rate_p, rate_u = rates(*column(c), x_y[c], y_y[c])
+                u = [get(row(2, a, b, c, v)) for b in middle]
+                rate_p, rate_u = rates([p[b][c] for b in middle], u, near_x[c], near_y[c], end[c])
                 for b in four:
                     rate[b][c] = rate_p[b]
                     put(row(2, a, b, c, v), rate_u[b])
+            end = [ends(p[b], [get(row(3, a, b, c, v)) for c in four]) for b in four]
+            near_x = [lanes(end[b][0], index(5, v)) for b in four]
+            near_y = [lanes(end[b][1], index(4, v)) for b in four]
             for b in four:
-                rate_p, rate_u = rates(*line(b), x_z[b], y_z[b])
+                u = [get(row(3, a, b, c, v)) for c in middle]
+                rate_p, rate_u = rates([p[b][c] for c in middle], u, near_x[b], near_y[b], end[b])
                 for c in four:
                     r = row(0, a, b, c, v)
                     put(r, dst[pl.ds(r, 8), :] + (rate[b][c] + rate_p[c]))
@@ -208,33 +217,29 @@
     high = chip // 2
     counts = jnp.zeros((1, CELLS), jnp.float32)
 
-    def take(pair, step_y, step_z):
+    def take(read, step_y, step_z):
         place = (high + 4 - step_y) % 4 * 2 + (low + step_z) % 2
         for half in range(2):
             base = place + 8 * half
             for m in range(ROWS // 8):
-                one[pl.ds(m * 8 * LAYERS + base, 8, stride=LAYERS), :] = pair[pl.ds(half * PART + m * 8, 8), :]
-            tail = pair[pl.ds(half * PART + ROWS, 8), :]
+                one[pl.ds(m * 8 * LAYERS + base, 8, stride=LAYERS), :] = read(half * PART + m * 8)
+            tail = read(half * PART + ROWS)
             for face in range(6):
                 index_ref[pl.ds(face * LAYERS + base, 1), :] = tail[face : face + 1].astype(jnp.int32)
 
-    take(pairs[0], 0, 0)
+    def reader(*sources):
+        return lambda r: functools.reduce(jnp.add, [source[pl.ds(r, 8), :] for source in sources])
+
+    take(reader(pairs[0]), 0, 0)
     for k, (zero, first) in enumerate(OFFSETS):
         if first is None:
-
-            @pl.when(core == 0)
-            def _():
-                take(pairs[1 + k], *zero[0])
-
-            @pl.when(core == 1)
-            def _():
-                take(pairs[5 + k], *zero[0])
+            take(reader(pairs[1 + k], pairs[5 + k]), *zero[0])
         else:
             for swapped in range(2):
                 on_zero = core == swapped
                 step_y = jnp.where(on_zero, zero[0][0], first[0][0])
                 step_z = jnp.where(on_zero, zero[0][1], first[0][1])
-                take(pairs[1 + 4 * swapped + k], step_y, step_z)
+                take(reader(pairs[1 + 4 * swapped + k]), step_y, step_z)
     for pair in pairs:
         counts = jnp.maximum(counts, pair[pl.ds(2 * PART, 1), :])
 

time: 49.6 us -> 48.8 us (0.984)
  Pallas kernels: 20.8 us -> 19.9 us
    pallas_call x1, Pallas kernels: 17.4 us -> 16.6 us  [shards(): pl.pallas_call(advance_kernel, out_shape=jax.ShapeDtypeStruct((3 * ROWS,...]
where the time goes in v3:
time: 48.8 us; the launch traced here: 48.6 us
  starting transfers between devices  25.5 us (52%)
  Pallas kernels  19.9 us (41%)
  local copies, waits for them, and re-layouts  1.22 us (2%)
  waiting for transfers between devices  1.19 us (2%)
  between operations  0.77 us (2%)
    pallas_call x1, Pallas kernels, shards(): pl.pallas_call(advance_kernel, out_shape=jax.ShapeDtypeStruct((3 * ROWS,...  16.6 us
    ppermute x4, starting transfers between devices, shards(): lax.ppermute(value, axes, one_way if entry[1] is None else swap)  10.7 us
    ppermute x4, starting transfers between devices, shards(): direct.append(lax.ppermute(pair if k < EARLY else late, axes, route(move)))  5.38 us
    ppermute x1, starting transfers between devices, shards(): own = lax.ppermute(late, axes, swap)  5.22 us
    ppermute x1, starting transfers between devices, shards(): lax.ppermute(step_counts, axes, route(lambda x, high, y, low, core: (x +...  2.83 us
    pallas_call x1, Pallas kernels, shards(): pl.pallas_call(prepare_kernel, out_shape=[jax.ShapeDtypeStruct((PAIR, CEL...  2.11 us
    ppermute x1, starting transfers between devices, shards(): other = lax.ppermute(state, axes, swap)  1.42 us
    pallas_call x1, Pallas kernels, shards(): pl.pallas_call(count_kernel, out_shape=jax.ShapeDtypeStruct((PAIR, CELLS)...  1.24 us
  transfers between devices with their start and end apart: 12, of which 1 were waited for; matrix products, arithmetic and copies ran while one was open for 0% of the time, Pallas kernels for 4%

profile of v3, /device:TPU:1, one launch (start us, length us, event | category | flops | bytes accessed | tf_op | source)
XLA Modules:
  0.0 48.6 jit_solution(5040039083162009540)
XLA Ops:
  0.0 1.4 %collective-permute-start.1 = (f32[256,128]{1,0:T(8,128)}, f32[256,128]{1,0:T(8,128)S(1)}, u32[]{:S(2)}, u32[]{:S(2)}) collective-permute-start(f32[256,128]{1,0:T(8,128)} %bitcast.4), channel_id=1, source_target_pairs={{0,1},{1,0},{2,3},{3,2},{4,5},{5,4},{6,7},{7,6},{8,9},{9,8},{10,11... | collective-permute-start | bytes 393224 | tf_op jit(solution)/shard_map/ppermute | solution.py:305
  1.4 0.0 collective-permute-start.2
  1.4 2.8 %collective-permute-start = (s32[1]{0:T(128)}, s32[1]{0:T(128)}, u32[]{:S(2)}, u32[]{:S(2)}) collective-permute-start(s32[1]{0:T(128)} %param.7), channel_id=1, source_target_pairs={{0,64},{1,65},{2,66},{3,67},{4,68},{5,69},{6,70},{7,71},{8,72},{9,... | collective-permute-start | bytes 20 | tf_op jit(solution)/shard_map/ppermute | solution.py:303
  4.9 0.0 collective-permute-done.2.near_other_ref
  4.9 0.0 copy-start.2
  5.0 0.0 collective-permute-done.1.other_ref
  5.0 0.6 %copy-done.2 = s32[6,1,128]{2,1,0:T(1,128)} copy-done((s32[6,1,128]{2,1,0:T(1,128)}, s32[6,1,128]{2,1,0:T(1,128)S(1)}, u32[]{:S(2)}) %copy-start.2) | copy-done | bytes 3096
  5.5 0.6 %copy-done.1 = f32[256,128]{1,0:T(8,128)} copy-done((f32[256,128]{1,0:T(8,128)}, f32[256,128]{1,0:T(8,128)S(1)}, u32[]{:S(2)}) %copy-start.1) | copy-done | bytes 131096
  6.2 2.1 %shard_map.55 = (f32[536,128]{1,0:T(8,128)}, f32[536,128]{1,0:T(8,128)}) custom-call(s32[1]{0:T(128)S(6)} %copy.9.step_ref, f32[256,128]{1,0:T(8,128)} %bitcast.5, f32[256,128]{1,0:T(8,128)} %copy-done.1, s32[6,1,128]{2,1,0:T(1,128)} %near_ref.1, s32[6,1,128]{2,1,0:T(1,128)} %copy-done.2, f32[64,64]{1,0:T(8,128)} %constant.4.clone.table_ref), custom_call_target="tpu_custom_call" | custom-call | tf_op jit(solution)/shard_map/pallas_call | solution.py:310
  8.3 0.0 collective-permute-done.far_ref
  8.3 1.2 %shard_map.56 = f32[536,128]{1,0:T(8,128)} custom-call(s32[1]{0:T(128)S(6)} %copy.9.step_ref, s32[1]{0:T(128)} %collective-permute-done.far_ref, f32[536,128]{1,0:T(8,128)} %get-tuple-element.7.pair_any), custom_call_target="tpu_custom_call", output_to_operand_aliasing={{}: (2, {})} | custom-call | tf_op jit(solution)/shard_map/pallas_call | solution.py:316
  9.6 0.7 %collective-permute-start.7 = (f32[536,128]{1,0:T(8,128)}, f32[536,128]{1,0:T(8,128)S(1)}, u32[]{:S(2)}, u32[]{:S(2)}) collective-permute-start(f32[536,128]{1,0:T(8,128)} %shard_map.56), channel_id=1, source_target_pairs={{0,18},{2,16},{4,22},{6,20},{8,26},{10,24},{12,30},{14,28},{16,2},... | collective-permute-start | bytes 823304 | tf_op jit(solution)/shard_map/ppermute | solution.py:334
  10.2 4.2 %collective-permute-start.6 = (f32[536,128]{1,0:T(8,128)}, f32[536,128]{1,0:T(8,128)S(1)}, u32[]{:S(2)}, u32[]{:S(2)}) collective-permute-start(f32[536,128]{1,0:T(8,128)} %shard_map.56), channel_id=1, source_target_pairs={{0,54},{1,47},{2,52},{3,45},{4,58},{5,35},{6,56},{7,33},{8,62},{9,... | collective-permute-start | bytes 823304 | tf_op jit(solution)/shard_map/ppermute | solution.py:334
  14.4 0.0 copy-done.3
  14.4 0.5 collective-permute-start.5
  14.9 0.1 collective-permute-start.4
  14.9 5.2 %collective-permute-start.3 = (f32[536,128]{1,0:T(8,128)}, f32[536,128]{1,0:T(8,128)S(1)}, u32[]{:S(2)}, u32[]{:S(2)}) collective-permute-start(f32[536,128]{1,0:T(8,128)} %shard_map.56), channel_id=1, source_target_pairs={{0,1},{1,0},{2,3},{3,2},{4,5},{5,4},{6,7},{7,6},{8,9},{9,8},{10,11... | collective-permute-start | bytes 823304 | tf_op jit(solution)/shard_map/ppermute | solution.py:335
  20.2 0.0 collective-permute-done.7.refs_4_
  20.2 1.3 %collective-permute-start.11 = (f32[536,128]{1,0:T(8,128)S(1)}, f32[536,128]{1,0:T(8,128)S(1)}, u32[]{:S(2)}, u32[]{:S(2)}) collective-permute-start(f32[536,128]{1,0:T(8,128)S(1)} %collective-permute-done.7.refs_4_), channel_id=1, source_target_pairs={{0,1},{2,3},{4,5},{6,7},{8,9},{10,11},{12,13},{14,15},{16,17},{18,... | collective-permute-start | bytes 823304 | tf_op jit(solution)/shard_map/ppermute | solution.py:337
  21.5 0.0 collective-permute-done.6.refs_3_
  21.5 7.1 %collective-permute-start.10 = (f32[536,128]{1,0:T(8,128)S(1)}, f32[536,128]{1,0:T(8,128)S(1)}, u32[]{:S(2)}, u32[]{:S(2)}) collective-permute-start(f32[536,128]{1,0:T(8,128)S(1)} %collective-permute-done.6.refs_3_), channel_id=1, source_target_pairs={{0,1},{1,0},{2,3},{3,2},{4,5},{5,4},{6,7},{7,6},{8,9},{9,8},{10,11... | collective-permute-start | bytes 823304 | tf_op jit(solution)/shard_map/ppermute | solution.py:337
  28.6 0.0 collective-permute-done.5.refs_2_
  28.6 0.0 collective-permute-start.9
  28.6 0.0 collective-permute-done.4.refs_1_
  28.6 2.2 %collective-permute-start.8 = (f32[536,128]{1,0:T(8,128)S(1)}, f32[536,128]{1,0:T(8,128)S(1)}, u32[]{:S(2)}, u32[]{:S(2)}) collective-permute-start(f32[536,128]{1,0:T(8,128)S(1)} %collective-permute-done.4.refs_1_), channel_id=1, source_target_pairs={{0,1},{1,0},{2,3},{3,2},{4,5},{5,4},{6,7},{7,6},{8,9},{9,8},{10,11... | collective-permute-start | bytes 823304 | tf_op jit(solution)/shard_map/ppermute | solution.py:337
  30.9 0.0 collective-permute-done.3.refs_0_
  30.9 0.0 collective-permute-done.11.refs_8_
  30.9 0.0 collective-permute-done.10.refs_7_
  30.9 0.0 collective-permute-done.9.refs_6_
  30.9 1.2 %collective-permute-done.8.refs_5_ = f32[536,128]{1,0:T(8,128)S(1)} collective-permute-done((f32[536,128]{1,0:T(8,128)S(1)}, f32[536,128]{1,0:T(8,128)S(1)}, u32[]{:S(2)}, u32[]{:S(2)}) %collective-permute-start.8) | collective-permute-done | bytes 274464 | tf_op jit(solution)/shard_map/ppermute | solution.py:337
  32.0 0.0 copy-done
  32.0 16.6 %shard_map.57 = f32[768,128]{1,0:T(8,128)} custom-call(f32[536,128]{1,0:T(8,128)S(1)} %collective-permute-done.3.refs_0_, f32[536,128]{1,0:T(8,128)S(1)} %collective-permute-done.4.refs_1_, f32[536,128]{1,0:T(8,128)S(1)} %collective-permute-done.5.refs_2_, f32[536,128]{1,0:T(8,128)S(1)} %collective-permute-done.6.refs_3_, ...), custom_call_target="tpu_custom_call" | custom-call | tf_op jit(solution)/shard_map/pallas_call | solution.py:341
  (3 shorter events, 0.0 us)
Async XLA Ops:
  0.0 5.0 %collective-permute-start.1 = (f32[256,128]{1,0:T(8,128)}, f32[256,128]{1,0:T(8,128)S(1)}, u32[]{:S(2)}, u32[]{:S(2)}) collective-permute-start(f32[256,128]{1,0:T(8,128)} %bitcast.4), channel_id=1, source_target_pairs={{0,1},{1,0},{2,3},{3,2},{4,5},{5,4},{6,7},{7,6},{8,9},{9,8},{10,11... | collective-permute-start | bytes 393224 | tf_op jit(solution)/shard_map/ppermute | solution.py:305
  1.4 3.5 %collective-permute-start.2 = (s32[6,1,128]{2,1,0:T(1,128)}, s32[6,1,128]{2,1,0:T(1,128)S(1)}, u32[]{:S(2)}, u32[]{:S(2)}) collective-permute-start(s32[6,1,128]{2,1,0:T(1,128)} %near_ref.1), channel_id=1, source_target_pairs={{0,1},{1,0},{2,3},{3,2},{4,5},{5,4},{6,7},{7,6},{8,9},{9,8},{10,11... | collective-permute-start | bytes 9224 | tf_op jit(solution)/shard_map/ppermute | solution.py:306
  1.4 6.9 %collective-permute-start = (s32[1]{0:T(128)}, s32[1]{0:T(128)}, u32[]{:S(2)}, u32[]{:S(2)}) collective-permute-start(s32[1]{0:T(128)} %param.7), channel_id=1, source_target_pairs={{0,64},{1,65},{2,66},{3,67},{4,68},{5,69},{6,70},{7,71},{8,72},{9,... | collective-permute-start | bytes 20 | tf_op jit(solution)/shard_map/ppermute | solution.py:303
  4.9 0.6 %copy-start.2 = (s32[6,1,128]{2,1,0:T(1,128)}, s32[6,1,128]{2,1,0:T(1,128)S(1)}, u32[]{:S(2)}) copy-start(s32[6,1,128]{2,1,0:T(1,128)S(1)} %collective-permute-done.2.near_other_ref) | copy-start | bytes 9220
  5.5 0.7 %copy-start.1 = (f32[256,128]{1,0:T(8,128)}, f32[256,128]{1,0:T(8,128)S(1)}, u32[]{:S(2)}) copy-start(f32[256,128]{1,0:T(8,128)S(1)} %collective-permute-done.1.other_ref) | copy-start | bytes 393220
  8.3 6.1 %copy-start.3 = (f32[536,128]{1,0:T(8,128)S(1)}, f32[536,128]{1,0:T(8,128)}, u32[]{:S(2)}) copy-start(f32[536,128]{1,0:T(8,128)} %get-tuple-element.8) | copy-start | bytes 823300
  8.3 23.7 %copy-start = (f32[64,64]{1,0:T(8,128)S(1)}, f32[64,64]{1,0:T(8,128)}, u32[]{:S(2)}) copy-start(f32[64,64]{1,0:T(8,128)} %constant.5.clone.refs_9_) | copy-start | bytes 49156
  9.6 10.6 %collective-permute-start.7 = (f32[536,128]{1,0:T(8,128)}, f32[536,128]{1,0:T(8,128)S(1)}, u32[]{:S(2)}, u32[]{:S(2)}) collective-permute-start(f32[536,128]{1,0:T(8,128)} %shard_map.56), channel_id=1, source_target_pairs={{0,18},{2,16},{4,22},{6,20},{8,26},{10,24},{12,30},{14,28},{16,2},... | collective-permute-start | bytes 823304 | tf_op jit(solution)/shard_map/ppermute | solution.py:334
  10.2 11.2 %collective-permute-start.6 = (f32[536,128]{1,0:T(8,128)}, f32[536,128]{1,0:T(8,128)S(1)}, u32[]{:S(2)}, u32[]{:S(2)}) collective-permute-start(f32[536,128]{1,0:T(8,128)} %shard_map.56), channel_id=1, source_target_pairs={{0,54},{1,47},{2,52},{3,45},{4,58},{5,35},{6,56},{7,33},{8,62},{9,... | collective-permute-start | bytes 823304 | tf_op jit(solution)/shard_map/ppermute | solution.py:334
  14.4 14.2 %collective-permute-start.5 = (f32[536,128]{1,0:T(8,128)S(1)}, f32[536,128]{1,0:T(8,128)S(1)}, u32[]{:S(2)}, u32[]{:S(2)}) collective-permute-start(f32[536,128]{1,0:T(8,128)S(1)} %copy-done.3), channel_id=1, source_target_pairs={{0,4},{1,13},{2,6},{3,15},{4,8},{5,1},{6,10},{7,3},{8,12},{9,5},{1... | collective-permute-start | bytes 823304 | tf_op jit(solution)/shard_map/ppermute | solution.py:334
  14.9 13.7 %collective-permute-start.4 = (f32[536,128]{1,0:T(8,128)S(1)}, f32[536,128]{1,0:T(8,128)S(1)}, u32[]{:S(2)}, u32[]{:S(2)}) collective-permute-start(f32[536,128]{1,0:T(8,128)S(1)} %copy-done.3), channel_id=1, source_target_pairs={{0,10},{1,9},{2,8},{3,11},{4,14},{5,13},{6,12},{7,15},{8,2},{9,1},... | collective-permute-start | bytes 823304 | tf_op jit(solution)/shard_map/ppermute | solution.py:334
  14.9 15.9 %collective-permute-start.3 = (f32[536,128]{1,0:T(8,128)}, f32[536,128]{1,0:T(8,128)S(1)}, u32[]{:S(2)}, u32[]{:S(2)}) collective-permute-start(f32[536,128]{1,0:T(8,128)} %shard_map.56), channel_id=1, source_target_pairs={{0,1},{1,0},{2,3},{3,2},{4,5},{5,4},{6,7},{7,6},{8,9},{9,8},{10,11... | collective-permute-start | bytes 823304 | tf_op jit(solution)/shard_map/ppermute | solution.py:335
  20.2 10.7 %collective-permute-start.11 = (f32[536,128]{1,0:T(8,128)S(1)}, f32[536,128]{1,0:T(8,128)S(1)}, u32[]{:S(2)}, u32[]{:S(2)}) collective-permute-start(f32[536,128]{1,0:T(8,128)S(1)} %collective-permute-done.7.refs_4_), channel_id=1, source_target_pairs={{0,1},{2,3},{4,5},{6,7},{8,9},{10,11},{12,13},{14,15},{16,17},{18,... | collective-permute-start | bytes 823304 | tf_op jit(solution)/shard_map/ppermute | solution.py:337
  21.5 9.4 %collective-permute-start.10 = (f32[536,128]{1,0:T(8,128)S(1)}, f32[536,128]{1,0:T(8,128)S(1)}, u32[]{:S(2)}, u32[]{:S(2)}) collective-permute-start(f32[536,128]{1,0:T(8,128)S(1)} %collective-permute-done.6.refs_3_), channel_id=1, source_target_pairs={{0,1},{1,0},{2,3},{3,2},{4,5},{5,4},{6,7},{7,6},{8,9},{9,8},{10,11... | collective-permute-start | bytes 823304 | tf_op jit(solution)/shard_map/ppermute | solution.py:337
  28.6 2.3 %collective-permute-start.9 = (f32[536,128]{1,0:T(8,128)S(1)}, f32[536,128]{1,0:T(8,128)S(1)}, u32[]{:S(2)}, u32[]{:S(2)}) collective-permute-start(f32[536,128]{1,0:T(8,128)S(1)} %collective-permute-done.5.refs_2_), channel_id=1, source_target_pairs={{0,1},{1,0},{2,3},{3,2},{4,5},{5,4},{6,7},{7,6},{8,9},{9,8},{10,11... | collective-permute-start | bytes 823304 | tf_op jit(solution)/shard_map/ppermute | solution.py:337
  28.6 3.4 %collective-permute-start.8 = (f32[536,128]{1,0:T(8,128)S(1)}, f32[536,128]{1,0:T(8,128)S(1)}, u32[]{:S(2)}, u32[]{:S(2)}) collective-permute-start(f32[536,128]{1,0:T(8,128)S(1)} %collective-permute-done.4.refs_1_), channel_id=1, source_target_pairs={{0,1},{1,0},{2,3},{3,2},{4,5},{5,4},{6,7},{7,6},{8,9},{9,8},{10,11... | collective-permute-start | bytes 823304 | tf_op jit(solution)/shard_map/ppermute | solution.py:337

commit v4 on v3

--- a/solution.py
+++ b/solution.py
@@ -270,7 +270,7 @@
 
     lax.fori_loop(0, DEGREE // 2, advance, 0)
 
-    group = 16
+    group = 8
 
     def combine(g, carry):
         total = [[None] * group for _ in range(3)]

time: 48.8 us -> 48.8 us (level)
  no operation moved by 1% of the time
where the time goes in v4:
time: 48.8 us; the launch traced here: 48.7 us
  starting transfers between devices  25.5 us (52%)
  Pallas kernels  20 us (41%)
  local copies, waits for them, and re-layouts  1.22 us (2%)
  waiting for transfers between devices  1.19 us (2%)
  between operations  0.77 us (2%)
    pallas_call x1, Pallas kernels, shards(): pl.pallas_call(advance_kernel, out_shape=jax.ShapeDtypeStruct((3 * ROWS,...  16.6 us
    ppermute x4, starting transfers between devices, shards(): lax.ppermute(value, axes, one_way if entry[1] is None else swap)  10.7 us
    ppermute x4, starting transfers between devices, shards(): direct.append(lax.ppermute(pair if k < EARLY else late, axes, route(move)))  5.38 us
    ppermute x1, starting transfers between devices, shards(): own = lax.ppermute(late, axes, swap)  5.22 us
    ppermute x1, starting transfers between devices, shards(): lax.ppermute(step_counts, axes, route(lambda x, high, y, low, core: (x +...  2.83 us
    pallas_call x1, Pallas kernels, shards(): pl.pallas_call(prepare_kernel, out_shape=[jax.ShapeDtypeStruct((PAIR, CEL...  2.11 us
    ppermute x1, starting transfers between devices, shards(): other = lax.ppermute(state, axes, swap)  1.42 us
    pallas_call x1, Pallas kernels, shards(): pl.pallas_call(count_kernel, out_shape=jax.ShapeDtypeStruct((PAIR, CELLS)...  1.24 us
  transfers between devices with their start and end apart: 12, of which 1 were waited for; matrix products, arithmetic and copies ran while one was open for 0% of the time, Pallas kernels for 4%

profile of v4, /device:TPU:1, one launch (start us, length us, event | category | flops | bytes accessed | tf_op | source)
XLA Modules:
  0.0 48.7 jit_solution(10493160451533189243)
XLA Ops:
  0.0 1.4 %collective-permute-start.1 = (f32[256,128]{1,0:T(8,128)}, f32[256,128]{1,0:T(8,128)S(1)}, u32[]{:S(2)}, u32[]{:S(2)}) collective-permute-start(f32[256,128]{1,0:T(8,128)} %bitcast.4), channel_id=1, source_target_pairs={{0,1},{1,0},{2,3},{3,2},{4,5},{5,4},{6,7},{7,6},{8,9},{9,8},{10,11... | collective-permute-start | bytes 393224 | tf_op jit(solution)/shard_map/ppermute | solution.py:305
  1.4 0.0 collective-permute-start.2
  1.4 2.8 %collective-permute-start = (s32[1]{0:T(128)}, s32[1]{0:T(128)}, u32[]{:S(2)}, u32[]{:S(2)}) collective-permute-start(s32[1]{0:T(128)} %param.7), channel_id=1, source_target_pairs={{0,64},{1,65},{2,66},{3,67},{4,68},{5,69},{6,70},{7,71},{8,72},{9,... | collective-permute-start | bytes 20 | tf_op jit(solution)/shard_map/ppermute | solution.py:303
  4.9 0.0 collective-permute-done.2.near_other_ref
  4.9 0.0 copy-start.2
  5.0 0.0 collective-permute-done.1.other_ref
  5.0 0.6 %copy-done.2 = s32[6,1,128]{2,1,0:T(1,128)} copy-done((s32[6,1,128]{2,1,0:T(1,128)}, s32[6,1,128]{2,1,0:T(1,128)S(1)}, u32[]{:S(2)}) %copy-start.2) | copy-done | bytes 3096
  5.5 0.6 %copy-done.1 = f32[256,128]{1,0:T(8,128)} copy-done((f32[256,128]{1,0:T(8,128)}, f32[256,128]{1,0:T(8,128)S(1)}, u32[]{:S(2)}) %copy-start.1) | copy-done | bytes 131096
  6.2 2.1 %shard_map.55 = (f32[536,128]{1,0:T(8,128)}, f32[536,128]{1,0:T(8,128)}) custom-call(s32[1]{0:T(128)S(6)} %copy.9.step_ref, f32[256,128]{1,0:T(8,128)} %bitcast.5, f32[256,128]{1,0:T(8,128)} %copy-done.1, s32[6,1,128]{2,1,0:T(1,128)} %near_ref.1, s32[6,1,128]{2,1,0:T(1,128)} %copy-done.2, f32[64,64]{1,0:T(8,128)} %constant.4.clone.table_ref), custom_call_target="tpu_custom_call" | custom-call | tf_op jit(solution)/shard_map/pallas_call | solution.py:310
  8.3 0.0 collective-permute-done.far_ref
  8.3 1.2 %shard_map.56 = f32[536,128]{1,0:T(8,128)} custom-call(s32[1]{0:T(128)S(6)} %copy.9.step_ref, s32[1]{0:T(128)} %collective-permute-done.far_ref, f32[536,128]{1,0:T(8,128)} %get-tuple-element.7.pair_any), custom_call_target="tpu_custom_call", output_to_operand_aliasing={{}: (2, {})} | custom-call | tf_op jit(solution)/shard_map/pallas_call | solution.py:316
  9.6 0.7 %collective-permute-start.7 = (f32[536,128]{1,0:T(8,128)}, f32[536,128]{1,0:T(8,128)S(1)}, u32[]{:S(2)}, u32[]{:S(2)}) collective-permute-start(f32[536,128]{1,0:T(8,128)} %shard_map.56), channel_id=1, source_target_pairs={{0,18},{2,16},{4,22},{6,20},{8,26},{10,24},{12,30},{14,28},{16,2},... | collective-permute-start | bytes 823304 | tf_op jit(solution)/shard_map/ppermute | solution.py:334
  10.2 4.2 %collective-permute-start.6 = (f32[536,128]{1,0:T(8,128)}, f32[536,128]{1,0:T(8,128)S(1)}, u32[]{:S(2)}, u32[]{:S(2)}) collective-permute-start(f32[536,128]{1,0:T(8,128)} %shard_map.56), channel_id=1, source_target_pairs={{0,54},{1,47},{2,52},{3,45},{4,58},{5,35},{6,56},{7,33},{8,62},{9,... | collective-permute-start | bytes 823304 | tf_op jit(solution)/shard_map/ppermute | solution.py:334
  14.4 0.0 copy-done.3
  14.4 0.5 collective-permute-start.5
  14.9 0.1 collective-permute-start.4
  14.9 5.2 %collective-permute-start.3 = (f32[536,128]{1,0:T(8,128)}, f32[536,128]{1,0:T(8,128)S(1)}, u32[]{:S(2)}, u32[]{:S(2)}) collective-permute-start(f32[536,128]{1,0:T(8,128)} %shard_map.56), channel_id=1, source_target_pairs={{0,1},{1,0},{2,3},{3,2},{4,5},{5,4},{6,7},{7,6},{8,9},{9,8},{10,11... | collective-permute-start | bytes 823304 | tf_op jit(solution)/shard_map/ppermute | solution.py:335
  20.2 0.0 collective-permute-done.7.refs_4_
  20.2 1.3 %collective-permute-start.11 = (f32[536,128]{1,0:T(8,128)S(1)}, f32[536,128]{1,0:T(8,128)S(1)}, u32[]{:S(2)}, u32[]{:S(2)}) collective-permute-start(f32[536,128]{1,0:T(8,128)S(1)} %collective-permute-done.7.refs_4_), channel_id=1, source_target_pairs={{0,1},{2,3},{4,5},{6,7},{8,9},{10,11},{12,13},{14,15},{16,17},{18,... | collective-permute-start | bytes 823304 | tf_op jit(solution)/shard_map/ppermute | solution.py:337
  21.5 0.0 collective-permute-done.6.refs_3_
  21.5 7.1 %collective-permute-start.10 = (f32[536,128]{1,0:T(8,128)S(1)}, f32[536,128]{1,0:T(8,128)S(1)}, u32[]{:S(2)}, u32[]{:S(2)}) collective-permute-start(f32[536,128]{1,0:T(8,128)S(1)} %collective-permute-done.6.refs_3_), channel_id=1, source_target_pairs={{0,1},{1,0},{2,3},{3,2},{4,5},{5,4},{6,7},{7,6},{8,9},{9,8},{10,11... | collective-permute-start | bytes 823304 | tf_op jit(solution)/shard_map/ppermute | solution.py:337
  28.6 0.0 collective-permute-done.5.refs_2_
  28.6 0.0 collective-permute-start.9
  28.6 0.0 collective-permute-done.4.refs_1_
  28.6 2.2 %collective-permute-start.8 = (f32[536,128]{1,0:T(8,128)S(1)}, f32[536,128]{1,0:T(8,128)S(1)}, u32[]{:S(2)}, u32[]{:S(2)}) collective-permute-start(f32[536,128]{1,0:T(8,128)S(1)} %collective-permute-done.4.refs_1_), channel_id=1, source_target_pairs={{0,1},{1,0},{2,3},{3,2},{4,5},{5,4},{6,7},{7,6},{8,9},{9,8},{10,11... | collective-permute-start | bytes 823304 | tf_op jit(solution)/shard_map/ppermute | solution.py:337
  30.9 0.0 collective-permute-done.3.refs_0_
  30.9 0.0 collective-permute-done.11.refs_8_
  30.9 0.0 collective-permute-done.10.refs_7_
  30.9 0.0 collective-permute-done.9.refs_6_
  30.9 1.2 %collective-permute-done.8.refs_5_ = f32[536,128]{1,0:T(8,128)S(1)} collective-permute-done((f32[536,128]{1,0:T(8,128)S(1)}, f32[536,128]{1,0:T(8,128)S(1)}, u32[]{:S(2)}, u32[]{:S(2)}) %collective-permute-start.8) | collective-permute-done | bytes 274464 | tf_op jit(solution)/shard_map/ppermute | solution.py:337
  32.0 0.0 copy-done
  32.0 16.6 %shard_map.57 = f32[768,128]{1,0:T(8,128)} custom-call(f32[536,128]{1,0:T(8,128)S(1)} %collective-permute-done.3.refs_0_, f32[536,128]{1,0:T(8,128)S(1)} %collective-permute-done.4.refs_1_, f32[536,128]{1,0:T(8,128)S(1)} %collective-permute-done.5.refs_2_, f32[536,128]{1,0:T(8,128)S(1)} %collective-permute-done.6.refs_3_, ...), custom_call_target="tpu_custom_call" | custom-call | tf_op jit(solution)/shard_map/pallas_call | solution.py:341
  (3 shorter events, 0.0 us)
Async XLA Ops:
  0.0 5.0 %collective-permute-start.1 = (f32[256,128]{1,0:T(8,128)}, f32[256,128]{1,0:T(8,128)S(1)}, u32[]{:S(2)}, u32[]{:S(2)}) collective-permute-start(f32[256,128]{1,0:T(8,128)} %bitcast.4), channel_id=1, source_target_pairs={{0,1},{1,0},{2,3},{3,2},{4,5},{5,4},{6,7},{7,6},{8,9},{9,8},{10,11... | collective-permute-start | bytes 393224 | tf_op jit(solution)/shard_map/ppermute | solution.py:305
  1.4 3.5 %collective-permute-start.2 = (s32[6,1,128]{2,1,0:T(1,128)}, s32[6,1,128]{2,1,0:T(1,128)S(1)}, u32[]{:S(2)}, u32[]{:S(2)}) collective-permute-start(s32[6,1,128]{2,1,0:T(1,128)} %near_ref.1), channel_id=1, source_target_pairs={{0,1},{1,0},{2,3},{3,2},{4,5},{5,4},{6,7},{7,6},{8,9},{9,8},{10,11... | collective-permute-start | bytes 9224 | tf_op jit(solution)/shard_map/ppermute | solution.py:306
  1.4 6.9 %collective-permute-start = (s32[1]{0:T(128)}, s32[1]{0:T(128)}, u32[]{:S(2)}, u32[]{:S(2)}) collective-permute-start(s32[1]{0:T(128)} %param.7), channel_id=1, source_target_pairs={{0,64},{1,65},{2,66},{3,67},{4,68},{5,69},{6,70},{7,71},{8,72},{9,... | collective-permute-start | bytes 20 | tf_op jit(solution)/shard_map/ppermute | solution.py:303
  4.9 0.6 %copy-start.2 = (s32[6,1,128]{2,1,0:T(1,128)}, s32[6,1,128]{2,1,0:T(1,128)S(1)}, u32[]{:S(2)}) copy-start(s32[6,1,128]{2,1,0:T(1,128)S(1)} %collective-permute-done.2.near_other_ref) | copy-start | bytes 9220
  5.5 0.7 %copy-start.1 = (f32[256,128]{1,0:T(8,128)}, f32[256,128]{1,0:T(8,128)S(1)}, u32[]{:S(2)}) copy-start(f32[256,128]{1,0:T(8,128)S(1)} %collective-permute-done.1.other_ref) | copy-start | bytes 393220
  8.3 6.1 %copy-start.3 = (f32[536,128]{1,0:T(8,128)S(1)}, f32[536,128]{1,0:T(8,128)}, u32[]{:S(2)}) copy-start(f32[536,128]{1,0:T(8,128)} %get-tuple-element.8) | copy-start | bytes 823300
  8.3 23.7 %copy-start = (f32[64,64]{1,0:T(8,128)S(1)}, f32[64,64]{1,0:T(8,128)}, u32[]{:S(2)}) copy-start(f32[64,64]{1,0:T(8,128)} %constant.5.clone.refs_9_) | copy-start | bytes 49156
  9.6 10.6 %collective-permute-start.7 = (f32[536,128]{1,0:T(8,128)}, f32[536,128]{1,0:T(8,128)S(1)}, u32[]{:S(2)}, u32[]{:S(2)}) collective-permute-start(f32[536,128]{1,0:T(8,128)} %shard_map.56), channel_id=1, source_target_pairs={{0,18},{2,16},{4,22},{6,20},{8,26},{10,24},{12,30},{14,28},{16,2},... | collective-permute-start | bytes 823304 | tf_op jit(solution)/shard_map/ppermute | solution.py:334
  10.2 11.2 %collective-permute-start.6 = (f32[536,128]{1,0:T(8,128)}, f32[536,128]{1,0:T(8,128)S(1)}, u32[]{:S(2)}, u32[]{:S(2)}) collective-permute-start(f32[536,128]{1,0:T(8,128)} %shard_map.56), channel_id=1, source_target_pairs={{0,54},{1,47},{2,52},{3,45},{4,58},{5,35},{6,56},{7,33},{8,62},{9,... | collective-permute-start | bytes 823304 | tf_op jit(solution)/shard_map/ppermute | solution.py:334
  14.4 14.2 %collective-permute-start.5 = (f32[536,128]{1,0:T(8,128)S(1)}, f32[536,128]{1,0:T(8,128)S(1)}, u32[]{:S(2)}, u32[]{:S(2)}) collective-permute-start(f32[536,128]{1,0:T(8,128)S(1)} %copy-done.3), channel_id=1, source_target_pairs={{0,4},{1,13},{2,6},{3,15},{4,8},{5,1},{6,10},{7,3},{8,12},{9,5},{1... | collective-permute-start | bytes 823304 | tf_op jit(solution)/shard_map/ppermute | solution.py:334
  14.9 13.7 %collective-permute-start.4 = (f32[536,128]{1,0:T(8,128)S(1)}, f32[536,128]{1,0:T(8,128)S(1)}, u32[]{:S(2)}, u32[]{:S(2)}) collective-permute-start(f32[536,128]{1,0:T(8,128)S(1)} %copy-done.3), channel_id=1, source_target_pairs={{0,10},{1,9},{2,8},{3,11},{4,14},{5,13},{6,12},{7,15},{8,2},{9,1},... | collective-permute-start | bytes 823304 | tf_op jit(solution)/shard_map/ppermute | solution.py:334
  14.9 15.9 %collective-permute-start.3 = (f32[536,128]{1,0:T(8,128)}, f32[536,128]{1,0:T(8,128)S(1)}, u32[]{:S(2)}, u32[]{:S(2)}) collective-permute-start(f32[536,128]{1,0:T(8,128)} %shard_map.56), channel_id=1, source_target_pairs={{0,1},{1,0},{2,3},{3,2},{4,5},{5,4},{6,7},{7,6},{8,9},{9,8},{10,11... | collective-permute-start | bytes 823304 | tf_op jit(solution)/shard_map/ppermute | solution.py:335
  20.2 10.7 %collective-permute-start.11 = (f32[536,128]{1,0:T(8,128)S(1)}, f32[536,128]{1,0:T(8,128)S(1)}, u32[]{:S(2)}, u32[]{:S(2)}) collective-permute-start(f32[536,128]{1,0:T(8,128)S(1)} %collective-permute-done.7.refs_4_), channel_id=1, source_target_pairs={{0,1},{2,3},{4,5},{6,7},{8,9},{10,11},{12,13},{14,15},{16,17},{18,... | collective-permute-start | bytes 823304 | tf_op jit(solution)/shard_map/ppermute | solution.py:337
  21.5 9.4 %collective-permute-start.10 = (f32[536,128]{1,0:T(8,128)S(1)}, f32[536,128]{1,0:T(8,128)S(1)}, u32[]{:S(2)}, u32[]{:S(2)}) collective-permute-start(f32[536,128]{1,0:T(8,128)S(1)} %collective-permute-done.6.refs_3_), channel_id=1, source_target_pairs={{0,1},{1,0},{2,3},{3,2},{4,5},{5,4},{6,7},{7,6},{8,9},{9,8},{10,11... | collective-permute-start | bytes 823304 | tf_op jit(solution)/shard_map/ppermute | solution.py:337
  28.6 2.3 %collective-permute-start.9 = (f32[536,128]{1,0:T(8,128)S(1)}, f32[536,128]{1,0:T(8,128)S(1)}, u32[]{:S(2)}, u32[]{:S(2)}) collective-permute-start(f32[536,128]{1,0:T(8,128)S(1)} %collective-permute-done.5.refs_2_), channel_id=1, source_target_pairs={{0,1},{1,0},{2,3},{3,2},{4,5},{5,4},{6,7},{7,6},{8,9},{9,8},{10,11... | collective-permute-start | bytes 823304 | tf_op jit(solution)/shard_map/ppermute | solution.py:337
  28.6 3.4 %collective-permute-start.8 = (f32[536,128]{1,0:T(8,128)S(1)}, f32[536,128]{1,0:T(8,128)S(1)}, u32[]{:S(2)}, u32[]{:S(2)}) collective-permute-start(f32[536,128]{1,0:T(8,128)S(1)} %collective-permute-done.4.refs_1_), channel_id=1, source_target_pairs={{0,1},{1,0},{2,3},{3,2},{4,5},{5,4},{6,7},{7,6},{8,9},{9,8},{10,11... | collective-permute-start | bytes 823304 | tf_op jit(solution)/shard_map/ppermute | solution.py:337
